TPU v7x, 512 devices: a whole 4x8x8 slice. The times are simulated.
512 devices in a mesh: section: 16 (over z_hi, x), dp: 32 (over y, z_lo, core).
Axes of the slice: x: 4, y: 8, z: 8 (z_hi: 4, z_lo: 2; z = z_hi * 2 + z_lo), core: 2. Of those that a mesh axis runs over, the one named last changes fastest.
Arguments:
- memory: bfloat16 [64, 8, 2048], P('dp', None, 'section'), may hold values from -8 to 8, as said below
- decoder_in: bfloat16 [64, 64, 2048], P('dp'), may hold values from -6 to 6
- key_weight: bfloat16 [16, 2048, 2048], P('section', None, 'dp'), may hold values from -0.125 to 0.125
- value_weight: bfloat16 [16, 2048, 2048], P('section', None, 'dp'), may hold values from -0.125 to 0.125
- top_grad: bfloat16 [64, 64, 2048], P('dp'), may hold values from -6 to 6
Outputs:
- memory_grad: float32 [512, 2048], P(('section', 'dp'))
Inputs may be any that keep to these rules, and one draw needn't show every extreme that they name: real-valued memory.
All inputs are finite; a program needn't handle non-finite values.
Results may differ from a plain program's by a relative error of at most 0.03.
Values may be sent and summed in bfloat16 or wider, within the bound.
No kernel may reach another device: no remote copies, remote signals or barrier semaphores. Data moves between devices by JAX's collectives and lax.ppermute only.
A program may use at most 64 MiB of HBM per device.

v0:
```python
import jax
import jax.numpy as jnp
from jax import lax
from jax.sharding import PartitionSpec as P

HEADS = 16
HEAD_DIMENSION = 128


def from_behind(block, axis, distance):
    devices = range(lax.axis_size(axis))
    route = [(i - distance, i) for i in devices if i - distance in devices]
    return lax.ppermute(block, axis, route)


def attend(hidden, keys, values):
    tokens = hidden.shape[0]
    scale = lax.rsqrt(jnp.mean(hidden * hidden, axis=-1, keepdims=True) + 1e-06)
    query_rows = (hidden * scale).reshape(tokens, HEADS, -1)
    key_head_split = keys.reshape(keys.shape[0], HEADS, -1)
    value_head_split = values.reshape(values.shape[0], HEADS, -1)
    score_matrix = jnp.einsum(
        "qig,rig->iqr", query_rows, key_head_split, precision=lax.Precision.HIGHEST
    ) / jnp.sqrt(jnp.float32(HEAD_DIMENSION))
    attention_weights = jax.nn.softmax(score_matrix, axis=-1)
    mixed_values = jnp.einsum(
        "xrl,lxz->rxz", attention_weights, value_head_split, precision=lax.Precision.HIGHEST
    )
    return hidden + mixed_values.reshape(tokens, -1)


def body(memory, decoder_in, key_weight, value_weight, top_grad):
    sections = lax.axis_size("section")
    replicas = lax.axis_size("dp")
    place = lax.axis_index("section")
    micro = decoder_in.shape[0]
    width = decoder_in.shape[2]
    tokens_mem = memory.shape[1]
    columns = key_weight.shape[2]
    both = jnp.concatenate([key_weight[0], value_weight[0]], axis=1)
    wide = lax.all_gather(memory, "section", axis=2, tiled=True)
    model = wide.shape[2]
    every = lax.all_gather(wide, "dp", axis=0, tiled=True)
    flat_piece = every.reshape(-1, model)
    result = jnp.dot(flat_piece, both, preferred_element_type=jnp.float32).astype(jnp.bfloat16)
    projected = result.reshape(every.shape[0], tokens_mem, 2 * columns)
    arrived = lax.all_to_all(projected, "dp", split_axis=0, concat_axis=2, tiled=True)
    arrived = arrived.reshape(micro, tokens_mem, replicas, 2, columns)
    keys = arrived[:, :, :, 0, :].reshape(micro, tokens_mem, width)
    values = arrived[:, :, :, 1, :].reshape(micro, tokens_mem, width)
    turns = sections + micro - 1

    def forward_turn(step, carry):
        incoming, stash = carry
        slot = step - place
        valid = (slot >= 0) & (slot < micro)
        index = jnp.clip(slot, 0, micro - 1)
        first = lax.dynamic_index_in_dim(decoder_in, index, 0, keepdims=False)
        entering = jnp.where(place == 0, first, incoming)
        key_now = lax.dynamic_index_in_dim(keys, index, 0, keepdims=False).astype(jnp.float32)
        value_now = lax.dynamic_index_in_dim(values, index, 0, keepdims=False).astype(jnp.float32)
        leaving = attend(entering.astype(jnp.float32), key_now, value_now).astype(jnp.bfloat16)
        previous = lax.dynamic_index_in_dim(stash, index, 0, keepdims=False)
        stash = lax.dynamic_update_index_in_dim(
            stash, jnp.where(valid, entering, previous), index, 0
        )
        incoming = from_behind(leaving, "section", 1)
        return (incoming, stash)

    start = (jnp.zeros_like(decoder_in[0]), jnp.zeros_like(decoder_in))
    unused, stash = lax.fori_loop(0, turns, forward_turn, start)

    def backward_turn(step, carry):
        incoming, key_grads, value_grads = carry
        slot = step - (sections - 1 - place)
        valid = (slot >= 0) & (slot < micro)
        index = jnp.clip(slot, 0, micro - 1)
        top = lax.dynamic_index_in_dim(top_grad, index, 0, keepdims=False)
        arriving = jnp.where(place == sections - 1, top, incoming)
        saved = lax.dynamic_index_in_dim(stash, index, 0, keepdims=False).astype(jnp.float32)
        key_now = lax.dynamic_index_in_dim(keys, index, 0, keepdims=False).astype(jnp.float32)
        value_now = lax.dynamic_index_in_dim(values, index, 0, keepdims=False).astype(jnp.float32)
        result, pull = jax.vjp(attend, saved, key_now, value_now)
        grad_hidden, grad_key, grad_value = pull(arriving.astype(jnp.float32))
        old_key = lax.dynamic_index_in_dim(key_grads, index, 0, keepdims=False)
        old_value = lax.dynamic_index_in_dim(value_grads, index, 0, keepdims=False)
        key_grads = lax.dynamic_update_index_in_dim(
            key_grads, jnp.where(valid, grad_key, old_key), index, 0
        )
        value_grads = lax.dynamic_update_index_in_dim(
            value_grads, jnp.where(valid, grad_value, old_value), index, 0
        )
        incoming = from_behind(grad_hidden.astype(jnp.bfloat16), "section", -1)
        return (incoming, key_grads, value_grads)

    empty = jnp.zeros(keys.shape, jnp.float32)
    begin = (jnp.zeros_like(top_grad[0]), empty, empty)
    unused_grad, key_grads, value_grads = lax.fori_loop(0, turns, backward_turn, begin)
    key_part = key_grads.astype(jnp.bfloat16).reshape(micro, tokens_mem, replicas, 1, columns)
    value_part = value_grads.astype(jnp.bfloat16).reshape(micro, tokens_mem, replicas, 1, columns)
    packed = jnp.concatenate([key_part, value_part], axis=3).reshape(
        micro, tokens_mem, replicas * 2 * columns
    )
    returned = lax.all_to_all(packed, "dp", split_axis=2, concat_axis=0, tiled=True)
    back_flat = returned.reshape(-1, 2 * columns)
    dims = (((1,), (1,)), ((), ()))
    terms = lax.dot_general(back_flat, both, dims, preferred_element_type=jnp.float32)
    return lax.psum_scatter(terms, ("section", "dp"), scatter_dimension=0, tiled=True)


def solution(mesh):
    placed = (
        P("dp", None, "section"),
        P("dp", None, None),
        P("section", None, "dp"),
        P("section", None, "dp"),
        P("dp", None, None),
    )
    return jax.shard_map(
        body, mesh=mesh, in_specs=placed, out_specs=P(("section", "dp"), None), check_vma=False
    )
```

profile of v0, /device:TPU:1, one launch (start us, length us, event | category | flops | bytes accessed | tf_op | source)
XLA Modules:
  0.0 1048.8 jit_solution(11041724177027402222)
XLA Ops:
  6.5 45.8 %all_gather.6 = bf16[2,8,2048]{2,1,0:T(8,128)(2,1)} all-gather(bf16[2,8,128]{2,1,0:T(8,128)(2,1)} %param.9), channel_id=1, replica_groups=mesh['section'=16,'dp'=32] {'section'}, dimensions={2}, use_global_device_ids=true | all-gather | bytes 69632 | tf_op jit(solution)/shard_map/all_gather | solution.py:41
  52.4 69.7 %all-gather.2.cloned.1.call-done = bf16[64,8,2048]{2,1,0:T(8,128)(2,1)} async-done(((bf16[2,8,2048]{2,1,0:T(8,128)(2,1)}), bf16[64,8,2048]{2,1,0:T(8,128)(2,1)}) %all-gather.2.cloned.1.call-update) | async-done | bytes 2097168 | tf_op jit(solution)/shard_map/all_gather | solution.py:43
  122.0 2.6 fusion.51
  125.4 6.7 all-to-all-start
  132.2 9.2 all-to-all-done
  143.5 214.0 %while.35 = (s32[]{:T(128)}, bf16[64,2048]{1,0:T(8,128)(2,1)S(1)}, bf16[2,64,2048]{2,1,0:T(8,128)(2,1)S(1)}, pred[]{:T(512)}, s32[]{:T(128)}, /*index=5*/bf16[2,...) while((s32[]{:T(128)}, bf16[64,2048]{1,0:T(8,128)(2,1)S(1)}, ...), condition=%wide.region_4.5_spmd, body=%wide.region_0.4_spmd.sunk | while | flops 26523720 | bytes 5207520 | solution.py:71
  145.2 3.1 collective-permute-start
  148.3 5.0 collective-permute-done
  155.0 4.1 collective-permute-start
  159.1 4.1 collective-permute-done
  164.9 4.1 collective-permute-start
  169.0 3.3 collective-permute-done
  173.9 3.8 collective-permute-start
  177.8 3.3 collective-permute-done
  182.7 5.4 collective-permute-start
  188.1 3.3 collective-permute-done
  193.1 7.1 collective-permute-start
  200.2 3.3 collective-permute-done
  205.1 6.9 collective-permute-start
  212.0 3.3 collective-permute-done
  216.9 6.9 collective-permute-start
  223.9 3.3 collective-permute-done
  228.8 6.9 collective-permute-start
  235.7 3.3 collective-permute-done
  240.6 6.9 collective-permute-start
  247.5 3.3 collective-permute-done
  252.5 7.0 collective-permute-start
  259.5 4.1 collective-permute-done
  265.3 7.6 collective-permute-start
  272.9 3.3 collective-permute-done
  277.8 11.2 %collective-permute-start = (bf16[64,2048]{1,0:T(8,128)(2,1)S(1)}, bf16[64,2048]{1,0:T(8,128)(2,1)S(1)}, u32[]{:S(2)}, u32[]{:S(2)}) collective-permute-start(bf16[64,2048]{1,0:T(8,128)(2,1)S(1)} %fusion.93), channel_id=1, source_target_pairs={{0,32},{32,64},{64,96},{96,128},{128,160},{160,192},{192,224},{224... | collective-permute-start | bytes 786440 | tf_op jit(solution)/shard_map/while/body/eval_jaxpr/ppermute | solution.py:13
  289.0 3.3 collective-permute-done
  293.9 10.6 %collective-permute-start = (bf16[64,2048]{1,0:T(8,128)(2,1)S(1)}, bf16[64,2048]{1,0:T(8,128)(2,1)S(1)}, u32[]{:S(2)}, u32[]{:S(2)}) collective-permute-start(bf16[64,2048]{1,0:T(8,128)(2,1)S(1)} %fusion.93), channel_id=1, source_target_pairs={{0,32},{32,64},{64,96},{96,128},{128,160},{160,192},{192,224},{224... | collective-permute-start | bytes 786440 | tf_op jit(solution)/shard_map/while/body/eval_jaxpr/ppermute | solution.py:13
  304.6 3.3 collective-permute-done
  309.5 10.0 collective-permute-start
  319.5 3.3 collective-permute-done
  324.5 15.0 %collective-permute-start = (bf16[64,2048]{1,0:T(8,128)(2,1)S(1)}, bf16[64,2048]{1,0:T(8,128)(2,1)S(1)}, u32[]{:S(2)}, u32[]{:S(2)}) collective-permute-start(bf16[64,2048]{1,0:T(8,128)(2,1)S(1)} %fusion.93), channel_id=1, source_target_pairs={{0,32},{32,64},{64,96},{96,128},{128,160},{160,192},{192,224},{224... | collective-permute-start | bytes 786440 | tf_op jit(solution)/shard_map/while/body/eval_jaxpr/ppermute | solution.py:13
  339.5 3.3 collective-permute-done
  344.4 9.8 collective-permute-start
  354.2 3.3 collective-permute-done
  357.6 314.6 %while.36 = (s32[]{:T(128)}, bf16[64,2048]{1,0:T(8,128)(2,1)S(1)}, bf16[2,8,2048]{2,1,0:T(8,128)(2,1)S(1)}, bf16[2,8,2048]{2,1,0:T(8,128)(2,1)S(1)}, pred[]{:T(5...) while((s32[]{:T(128)}, bf16[64,2048]{1,0:T(8,128)(2,1)S(1)}, ...), condition=%wide.region_11.12_spmd, body=%wide.region_5.11_spmd.sunk | while | flops 54985092 | bytes 10278138 | solution.py:98
  362.4 17.3 %collective-permute-done.1 = bf16[64,2048]{1,0:T(8,128)(2,1)S(1)} collective-permute-done((bf16[64,2048]{1,0:T(8,128)(2,1)S(1)}, bf16[64,2048]{1,0:T(8,128)(2,1)S(1)}, u32[]{:S(2)}, u32[]{:S(2)}) %collective-permute-start.1) | collective-permute-done | bytes 262176 | tf_op jit(solution)/shard_map/while/body/eval_jaxpr/ppermute | solution.py:13
  384.5 9.1 collective-permute-done.1
  398.4 14.5 %collective-permute-done.1 = bf16[64,2048]{1,0:T(8,128)(2,1)S(1)} collective-permute-done((bf16[64,2048]{1,0:T(8,128)(2,1)S(1)}, bf16[64,2048]{1,0:T(8,128)(2,1)S(1)}, u32[]{:S(2)}, u32[]{:S(2)}) %collective-permute-start.1) | collective-permute-done | bytes 262176 | tf_op jit(solution)/shard_map/while/body/eval_jaxpr/ppermute | solution.py:13
  417.7 12.4 %collective-permute-done.1 = bf16[64,2048]{1,0:T(8,128)(2,1)S(1)} collective-permute-done((bf16[64,2048]{1,0:T(8,128)(2,1)S(1)}, bf16[64,2048]{1,0:T(8,128)(2,1)S(1)}, u32[]{:S(2)}, u32[]{:S(2)}) %collective-permute-start.1) | collective-permute-done | bytes 262176 | tf_op jit(solution)/shard_map/while/body/eval_jaxpr/ppermute | solution.py:13
  434.9 13.5 %collective-permute-done.1 = bf16[64,2048]{1,0:T(8,128)(2,1)S(1)} collective-permute-done((bf16[64,2048]{1,0:T(8,128)(2,1)S(1)}, bf16[64,2048]{1,0:T(8,128)(2,1)S(1)}, u32[]{:S(2)}, u32[]{:S(2)}) %collective-permute-start.1) | collective-permute-done | bytes 262176 | tf_op jit(solution)/shard_map/while/body/eval_jaxpr/ppermute | solution.py:13
  453.3 13.6 %collective-permute-done.1 = bf16[64,2048]{1,0:T(8,128)(2,1)S(1)} collective-permute-done((bf16[64,2048]{1,0:T(8,128)(2,1)S(1)}, bf16[64,2048]{1,0:T(8,128)(2,1)S(1)}, u32[]{:S(2)}, u32[]{:S(2)}) %collective-permute-start.1) | collective-permute-done | bytes 262176 | tf_op jit(solution)/shard_map/while/body/eval_jaxpr/ppermute | solution.py:13
  471.6 16.8 %collective-permute-done.1 = bf16[64,2048]{1,0:T(8,128)(2,1)S(1)} collective-permute-done((bf16[64,2048]{1,0:T(8,128)(2,1)S(1)}, bf16[64,2048]{1,0:T(8,128)(2,1)S(1)}, u32[]{:S(2)}, u32[]{:S(2)}) %collective-permute-start.1) | collective-permute-done | bytes 262176 | tf_op jit(solution)/shard_map/while/body/eval_jaxpr/ppermute | solution.py:13
  493.3 21.4 %collective-permute-done.1 = bf16[64,2048]{1,0:T(8,128)(2,1)S(1)} collective-permute-done((bf16[64,2048]{1,0:T(8,128)(2,1)S(1)}, bf16[64,2048]{1,0:T(8,128)(2,1)S(1)}, u32[]{:S(2)}, u32[]{:S(2)}) %collective-permute-start.1) | collective-permute-done | bytes 262176 | tf_op jit(solution)/shard_map/while/body/eval_jaxpr/ppermute | solution.py:13
  519.5 12.1 %collective-permute-done.1 = bf16[64,2048]{1,0:T(8,128)(2,1)S(1)} collective-permute-done((bf16[64,2048]{1,0:T(8,128)(2,1)S(1)}, bf16[64,2048]{1,0:T(8,128)(2,1)S(1)}, u32[]{:S(2)}, u32[]{:S(2)}) %collective-permute-start.1) | collective-permute-done | bytes 262176 | tf_op jit(solution)/shard_map/while/body/eval_jaxpr/ppermute | solution.py:13
  536.4 4.8 collective-permute-done.1
  546.0 20.6 %collective-permute-done.1 = bf16[64,2048]{1,0:T(8,128)(2,1)S(1)} collective-permute-done((bf16[64,2048]{1,0:T(8,128)(2,1)S(1)}, bf16[64,2048]{1,0:T(8,128)(2,1)S(1)}, u32[]{:S(2)}, u32[]{:S(2)}) %collective-permute-start.1) | collective-permute-done | bytes 262176 | tf_op jit(solution)/shard_map/while/body/eval_jaxpr/ppermute | solution.py:13
  571.5 13.2 %collective-permute-done.1 = bf16[64,2048]{1,0:T(8,128)(2,1)S(1)} collective-permute-done((bf16[64,2048]{1,0:T(8,128)(2,1)S(1)}, bf16[64,2048]{1,0:T(8,128)(2,1)S(1)}, u32[]{:S(2)}, u32[]{:S(2)}) %collective-permute-start.1) | collective-permute-done | bytes 262176 | tf_op jit(solution)/shard_map/while/body/eval_jaxpr/ppermute | solution.py:13
  589.5 4.8 collective-permute-done.1
  599.1 20.0 %collective-permute-done.1 = bf16[64,2048]{1,0:T(8,128)(2,1)S(1)} collective-permute-done((bf16[64,2048]{1,0:T(8,128)(2,1)S(1)}, bf16[64,2048]{1,0:T(8,128)(2,1)S(1)}, u32[]{:S(2)}, u32[]{:S(2)}) %collective-permute-start.1) | collective-permute-done | bytes 262176 | tf_op jit(solution)/shard_map/while/body/eval_jaxpr/ppermute | solution.py:13
  624.0 12.5 %collective-permute-done.1 = bf16[64,2048]{1,0:T(8,128)(2,1)S(1)} collective-permute-done((bf16[64,2048]{1,0:T(8,128)(2,1)S(1)}, bf16[64,2048]{1,0:T(8,128)(2,1)S(1)}, u32[]{:S(2)}, u32[]{:S(2)}) %collective-permute-start.1) | collective-permute-done | bytes 262176 | tf_op jit(solution)/shard_map/while/body/eval_jaxpr/ppermute | solution.py:13
  641.4 4.8 collective-permute-done.1
  651.0 21.1 %collective-permute-done.1 = bf16[64,2048]{1,0:T(8,128)(2,1)S(1)} collective-permute-done((bf16[64,2048]{1,0:T(8,128)(2,1)S(1)}, bf16[64,2048]{1,0:T(8,128)(2,1)S(1)}, u32[]{:S(2)}, u32[]{:S(2)}) %collective-permute-start.1) | collective-permute-done | bytes 262176 | tf_op jit(solution)/shard_map/while/body/eval_jaxpr/ppermute | solution.py:13
  673.2 2.5 copy.58
  675.8 2.2 reshape.185
  678.0 42.0 %all_to_all.30 = bf16[32,2,1024]{2,1,0:T(2,128)(2,1)S(1)} all-to-all(bf16[32,2,1024]{2,1,0:T(2,128)(2,1)S(1)} %reshape.185), channel_id=1, replica_groups=mesh['section'=16,'dp'=32] {'dp'}, dimensions={0} | all-to-all | bytes 262144 | tf_op jit(solution)/shard_map/all_to_all | solution.py:104
  720.0 2.4 reshape.186
  724.5 2.7 fusion.54
  727.2 313.3 %all-reduce.3.cloned.1.call-done = f32[512,2048]{1,0:T(8,128)} async-done(((f32[512,2048]{1,0:T(8,128)}), f32[512,2048]{1,0:T(8,128)}) %all-reduce.3.cloned.1.call-update) | async-done | bytes 4194320
  (453 shorter events, 115.1 us)
Async XLA Ops:
  6.5 115.5 %all-gather.2.cloned.1.call-start = ((), (), s32[]{:S(2)}) async-start(), calls=%async_computation.2 | async-start | bytes 2162688 | tf_op jit(solution)/shard_map/all_gather | solution.py:43
  124.6 18.8 %copy-start = (bf16[2,64,2048]{2,1,0:T(8,128)(2,1)S(1)}, bf16[2,64,2048]{2,1,0:T(8,128)(2,1)}, u32[]{:S(2)}) copy-start(bf16[2,64,2048]{2,1,0:T(8,128)(2,1)} %param.10) | copy-start | bytes 1572868
  125.4 16.0 %all-to-all-start = ((bf16[64,8,128]{2,1,0:T(8,128)(2,1)}), bf16[64,8,128]{2,1,0:T(8,128)(2,1)S(1)}, u32[]{:S(2)}, u32[]{:S(2)}) async-start(bf16[64,8,128]{2,1,0:T(8,128)(2,1)} %bitcast.20), calls=%async_computation | async-start | bytes 262144 | tf_op jit(solution)/shard_map/all_to_all | solution.py:47
  132.1 908.4 %all-reduce.3.cloned.1.call-start = ((), (), s32[]{:S(2)}) async-start(), calls=%async_computation.3 | async-start | bytes 8388608
  143.5 214.1 %copy-start.1 = (bf16[2,64,2048]{2,1,0:T(8,128)(2,1)S(1)}, bf16[2,64,2048]{2,1,0:T(8,128)(2,1)}, u32[]{:S(2)}) copy-start(bf16[2,64,2048]{2,1,0:T(8,128)(2,1)} %param.13) | copy-start | bytes 1572868
  145.2 8.1 collective-permute-start
  155.0 8.3 collective-permute-start
  164.9 7.4 collective-permute-start
  173.9 7.1 collective-permute-start
  182.7 8.7 collective-permute-start
  193.1 10.4 collective-permute-start
  205.1 10.1 collective-permute-start
  216.9 10.2 collective-permute-start
  228.8 10.2 collective-permute-start
  240.6 10.2 collective-permute-start
  252.5 11.2 %collective-permute-start = (bf16[64,2048]{1,0:T(8,128)(2,1)S(1)}, bf16[64,2048]{1,0:T(8,128)(2,1)S(1)}, u32[]{:S(2)}, u32[]{:S(2)}) collective-permute-start(bf16[64,2048]{1,0:T(8,128)(2,1)S(1)} %fusion.93), channel_id=1, source_target_pairs={{0,32},{32,64},{64,96},{96,128},{128,160},{160,192},{192,224},{224... | collective-permute-start | bytes 786440 | tf_op jit(solution)/shard_map/while/body/eval_jaxpr/ppermute | solution.py:13
  265.3 10.9 %collective-permute-start = (bf16[64,2048]{1,0:T(8,128)(2,1)S(1)}, bf16[64,2048]{1,0:T(8,128)(2,1)S(1)}, u32[]{:S(2)}, u32[]{:S(2)}) collective-permute-start(bf16[64,2048]{1,0:T(8,128)(2,1)S(1)} %fusion.93), channel_id=1, source_target_pairs={{0,32},{32,64},{64,96},{96,128},{128,160},{160,192},{192,224},{224... | collective-permute-start | bytes 786440 | tf_op jit(solution)/shard_map/while/body/eval_jaxpr/ppermute | solution.py:13
  277.8 14.5 %collective-permute-start = (bf16[64,2048]{1,0:T(8,128)(2,1)S(1)}, bf16[64,2048]{1,0:T(8,128)(2,1)S(1)}, u32[]{:S(2)}, u32[]{:S(2)}) collective-permute-start(bf16[64,2048]{1,0:T(8,128)(2,1)S(1)} %fusion.93), channel_id=1, source_target_pairs={{0,32},{32,64},{64,96},{96,128},{128,160},{160,192},{192,224},{224... | collective-permute-start | bytes 786440 | tf_op jit(solution)/shard_map/while/body/eval_jaxpr/ppermute | solution.py:13
  293.9 13.9 %collective-permute-start = (bf16[64,2048]{1,0:T(8,128)(2,1)S(1)}, bf16[64,2048]{1,0:T(8,128)(2,1)S(1)}, u32[]{:S(2)}, u32[]{:S(2)}) collective-permute-start(bf16[64,2048]{1,0:T(8,128)(2,1)S(1)} %fusion.93), channel_id=1, source_target_pairs={{0,32},{32,64},{64,96},{96,128},{128,160},{160,192},{192,224},{224... | collective-permute-start | bytes 786440 | tf_op jit(solution)/shard_map/while/body/eval_jaxpr/ppermute | solution.py:13
  309.5 13.3 %collective-permute-start = (bf16[64,2048]{1,0:T(8,128)(2,1)S(1)}, bf16[64,2048]{1,0:T(8,128)(2,1)S(1)}, u32[]{:S(2)}, u32[]{:S(2)}) collective-permute-start(bf16[64,2048]{1,0:T(8,128)(2,1)S(1)} %fusion.93), channel_id=1, source_target_pairs={{0,32},{32,64},{64,96},{96,128},{128,160},{160,192},{192,224},{224... | collective-permute-start | bytes 786440 | tf_op jit(solution)/shard_map/while/body/eval_jaxpr/ppermute | solution.py:13
  324.5 18.3 %collective-permute-start = (bf16[64,2048]{1,0:T(8,128)(2,1)S(1)}, bf16[64,2048]{1,0:T(8,128)(2,1)S(1)}, u32[]{:S(2)}, u32[]{:S(2)}) collective-permute-start(bf16[64,2048]{1,0:T(8,128)(2,1)S(1)} %fusion.93), channel_id=1, source_target_pairs={{0,32},{32,64},{64,96},{96,128},{128,160},{160,192},{192,224},{224... | collective-permute-start | bytes 786440 | tf_op jit(solution)/shard_map/while/body/eval_jaxpr/ppermute | solution.py:13
  344.4 13.1 %collective-permute-start = (bf16[64,2048]{1,0:T(8,128)(2,1)S(1)}, bf16[64,2048]{1,0:T(8,128)(2,1)S(1)}, u32[]{:S(2)}, u32[]{:S(2)}) collective-permute-start(bf16[64,2048]{1,0:T(8,128)(2,1)S(1)} %fusion.93), channel_id=1, source_target_pairs={{0,32},{32,64},{64,96},{96,128},{128,160},{160,192},{192,224},{224... | collective-permute-start | bytes 786440 | tf_op jit(solution)/shard_map/while/body/eval_jaxpr/ppermute | solution.py:13
  360.0 19.6 %collective-permute-start.1 = (bf16[64,2048]{1,0:T(8,128)(2,1)S(1)}, bf16[64,2048]{1,0:T(8,128)(2,1)S(1)}, u32[]{:S(2)}, u32[]{:S(2)}) collective-permute-start(bf16[64,2048]{1,0:T(8,128)(2,1)S(1)} %fusion.104), channel_id=1, source_target_pairs={{32,0},{64,32},{96,64},{128,96},{160,128},{192,160},{224,192},{256... | collective-permute-start | bytes 786440 | tf_op jit(solution)/shard_map/while/body/eval_jaxpr/ppermute | solution.py:13
  382.1 11.4 %collective-permute-start.1 = (bf16[64,2048]{1,0:T(8,128)(2,1)S(1)}, bf16[64,2048]{1,0:T(8,128)(2,1)S(1)}, u32[]{:S(2)}, u32[]{:S(2)}) collective-permute-start(bf16[64,2048]{1,0:T(8,128)(2,1)S(1)} %fusion.104), channel_id=1, source_target_pairs={{32,0},{64,32},{96,64},{128,96},{160,128},{192,160},{224,192},{256... | collective-permute-start | bytes 786440 | tf_op jit(solution)/shard_map/while/body/eval_jaxpr/ppermute | solution.py:13
  396.0 16.8 %collective-permute-start.1 = (bf16[64,2048]{1,0:T(8,128)(2,1)S(1)}, bf16[64,2048]{1,0:T(8,128)(2,1)S(1)}, u32[]{:S(2)}, u32[]{:S(2)}) collective-permute-start(bf16[64,2048]{1,0:T(8,128)(2,1)S(1)} %fusion.104), channel_id=1, source_target_pairs={{32,0},{64,32},{96,64},{128,96},{160,128},{192,160},{224,192},{256... | collective-permute-start | bytes 786440 | tf_op jit(solution)/shard_map/while/body/eval_jaxpr/ppermute | solution.py:13
  415.3 14.7 %collective-permute-start.1 = (bf16[64,2048]{1,0:T(8,128)(2,1)S(1)}, bf16[64,2048]{1,0:T(8,128)(2,1)S(1)}, u32[]{:S(2)}, u32[]{:S(2)}) collective-permute-start(bf16[64,2048]{1,0:T(8,128)(2,1)S(1)} %fusion.104), channel_id=1, source_target_pairs={{32,0},{64,32},{96,64},{128,96},{160,128},{192,160},{224,192},{256... | collective-permute-start | bytes 786440 | tf_op jit(solution)/shard_map/while/body/eval_jaxpr/ppermute | solution.py:13
  432.6 15.8 %collective-permute-start.1 = (bf16[64,2048]{1,0:T(8,128)(2,1)S(1)}, bf16[64,2048]{1,0:T(8,128)(2,1)S(1)}, u32[]{:S(2)}, u32[]{:S(2)}) collective-permute-start(bf16[64,2048]{1,0:T(8,128)(2,1)S(1)} %fusion.104), channel_id=1, source_target_pairs={{32,0},{64,32},{96,64},{128,96},{160,128},{192,160},{224,192},{256... | collective-permute-start | bytes 786440 | tf_op jit(solution)/shard_map/while/body/eval_jaxpr/ppermute | solution.py:13
  450.9 15.9 %collective-permute-start.1 = (bf16[64,2048]{1,0:T(8,128)(2,1)S(1)}, bf16[64,2048]{1,0:T(8,128)(2,1)S(1)}, u32[]{:S(2)}, u32[]{:S(2)}) collective-permute-start(bf16[64,2048]{1,0:T(8,128)(2,1)S(1)} %fusion.104), channel_id=1, source_target_pairs={{32,0},{64,32},{96,64},{128,96},{160,128},{192,160},{224,192},{256... | collective-permute-start | bytes 786440 | tf_op jit(solution)/shard_map/while/body/eval_jaxpr/ppermute | solution.py:13
  469.3 19.1 %collective-permute-start.1 = (bf16[64,2048]{1,0:T(8,128)(2,1)S(1)}, bf16[64,2048]{1,0:T(8,128)(2,1)S(1)}, u32[]{:S(2)}, u32[]{:S(2)}) collective-permute-start(bf16[64,2048]{1,0:T(8,128)(2,1)S(1)} %fusion.104), channel_id=1, source_target_pairs={{32,0},{64,32},{96,64},{128,96},{160,128},{192,160},{224,192},{256... | collective-permute-start | bytes 786440 | tf_op jit(solution)/shard_map/while/body/eval_jaxpr/ppermute | solution.py:13
  490.9 23.8 %collective-permute-start.1 = (bf16[64,2048]{1,0:T(8,128)(2,1)S(1)}, bf16[64,2048]{1,0:T(8,128)(2,1)S(1)}, u32[]{:S(2)}, u32[]{:S(2)}) collective-permute-start(bf16[64,2048]{1,0:T(8,128)(2,1)S(1)} %fusion.104), channel_id=1, source_target_pairs={{32,0},{64,32},{96,64},{128,96},{160,128},{192,160},{224,192},{256... | collective-permute-start | bytes 786440 | tf_op jit(solution)/shard_map/while/body/eval_jaxpr/ppermute | solution.py:13
  517.2 14.4 %collective-permute-start.1 = (bf16[64,2048]{1,0:T(8,128)(2,1)S(1)}, bf16[64,2048]{1,0:T(8,128)(2,1)S(1)}, u32[]{:S(2)}, u32[]{:S(2)}) collective-permute-start(bf16[64,2048]{1,0:T(8,128)(2,1)S(1)} %fusion.104), channel_id=1, source_target_pairs={{32,0},{64,32},{96,64},{128,96},{160,128},{192,160},{224,192},{256... | collective-permute-start | bytes 786440 | tf_op jit(solution)/shard_map/while/body/eval_jaxpr/ppermute | solution.py:13
  534.1 7.1 collective-permute-start.1
  543.7 23.0 %collective-permute-start.1 = (bf16[64,2048]{1,0:T(8,128)(2,1)S(1)}, bf16[64,2048]{1,0:T(8,128)(2,1)S(1)}, u32[]{:S(2)}, u32[]{:S(2)}) collective-permute-start(bf16[64,2048]{1,0:T(8,128)(2,1)S(1)} %fusion.104), channel_id=1, source_target_pairs={{32,0},{64,32},{96,64},{128,96},{160,128},{192,160},{224,192},{256... | collective-permute-start | bytes 786440 | tf_op jit(solution)/shard_map/while/body/eval_jaxpr/ppermute | solution.py:13
  569.2 15.5 %collective-permute-start.1 = (bf16[64,2048]{1,0:T(8,128)(2,1)S(1)}, bf16[64,2048]{1,0:T(8,128)(2,1)S(1)}, u32[]{:S(2)}, u32[]{:S(2)}) collective-permute-start(bf16[64,2048]{1,0:T(8,128)(2,1)S(1)} %fusion.104), channel_id=1, source_target_pairs={{32,0},{64,32},{96,64},{128,96},{160,128},{192,160},{224,192},{256... | collective-permute-start | bytes 786440 | tf_op jit(solution)/shard_map/while/body/eval_jaxpr/ppermute | solution.py:13
  587.2 7.1 collective-permute-start.1
  596.8 22.4 %collective-permute-start.1 = (bf16[64,2048]{1,0:T(8,128)(2,1)S(1)}, bf16[64,2048]{1,0:T(8,128)(2,1)S(1)}, u32[]{:S(2)}, u32[]{:S(2)}) collective-permute-start(bf16[64,2048]{1,0:T(8,128)(2,1)S(1)} %fusion.104), channel_id=1, source_target_pairs={{32,0},{64,32},{96,64},{128,96},{160,128},{192,160},{224,192},{256... | collective-permute-start | bytes 786440 | tf_op jit(solution)/shard_map/while/body/eval_jaxpr/ppermute | solution.py:13
  621.7 14.9 %collective-permute-start.1 = (bf16[64,2048]{1,0:T(8,128)(2,1)S(1)}, bf16[64,2048]{1,0:T(8,128)(2,1)S(1)}, u32[]{:S(2)}, u32[]{:S(2)}) collective-permute-start(bf16[64,2048]{1,0:T(8,128)(2,1)S(1)} %fusion.104), channel_id=1, source_target_pairs={{32,0},{64,32},{96,64},{128,96},{160,128},{192,160},{224,192},{256... | collective-permute-start | bytes 786440 | tf_op jit(solution)/shard_map/while/body/eval_jaxpr/ppermute | solution.py:13
  639.0 7.1 collective-permute-start.1
  648.6 23.5 %collective-permute-start.1 = (bf16[64,2048]{1,0:T(8,128)(2,1)S(1)}, bf16[64,2048]{1,0:T(8,128)(2,1)S(1)}, u32[]{:S(2)}, u32[]{:S(2)}) collective-permute-start(bf16[64,2048]{1,0:T(8,128)(2,1)S(1)} %fusion.104), channel_id=1, source_target_pairs={{32,0},{64,32},{96,64},{128,96},{160,128},{192,160},{224,192},{256... | collective-permute-start | bytes 786440 | tf_op jit(solution)/shard_map/while/body/eval_jaxpr/ppermute | solution.py:13
  720.0 4.5 copy-start.2
  720.0 4.5 copy-start.3
Sparse Core Ops, SparseCore 0:
  52.5 69.4 all-gather.1
  727.3 313.1 all-reduce.2
where the time goes:
time: 1050 us
  waiting for transfers between devices  684 us (65%)
  starting transfers between devices  155 us (15%)
  blocking collectives  87.9 us (8%)
  matrix products  71.9 us (7%)
  other arithmetic  17.4 us (2%)
  local copies, waits for them, and re-layouts  16.1 us (2%)
  between operations  13.6 us (1%)
    unnamed x3, waiting for transfers between devices  313 us
    ppermute x34, waiting for transfers between devices, from_behind(): return lax.ppermute(block, axis, route)  292 us
    ppermute x34, starting transfers between devices, from_behind(): return lax.ppermute(block, axis, route)  148 us
    all_gather x1, waiting for transfers between devices, body(): every = lax.all_gather(wide, 'dp', axis=0, tiled=True)  69.7 us
    all_gather x1, blocking collectives, body(): wide = lax.all_gather(memory, 'section', axis=2, tiled=True)  45.8 us
    dot_general x68, matrix products, attend(): jnp.einsum('qig,rig->iqr', query_rows, key_head_split, precision=lax.Prec...  45.7 us
    all_to_all x1, blocking collectives, body(): lax.all_to_all(packed, 'dp', split_axis=2, concat_axis=0, tiled=True)  42 us
  transfers between devices with their start and end apart: 37, of which 37 were waited for; matrix products, arithmetic and copies ran while one was open for 2% of the time, Pallas kernels for 0%

commit v1 on v0

v1 whole, which is shorter than its diff:
```python
import functools

import jax
import jax.numpy as jnp
from jax import lax
from jax.experimental import pallas as pl
from jax.experimental.pallas import tpu as pltpu
from jax.sharding import Mesh
from jax.sharding import PartitionSpec as P

HEADS = 16
HEAD_DIMENSION = 128
SECTIONS = 16
MEM = 8
TOKENS = 8
WIDTH = HEADS * HEAD_DIMENSION
LANES = MEM * HEADS
SECTION = ("zh", "x")
DP = ("y", "zl", "c")
RING = ("zh", "x", "y")
F32 = jnp.float32
BF16 = jnp.bfloat16


def wide_dot(a, b):
    return lax.dot_general(a, b, (((1,), (0,)), ((), ())), preferred_element_type=F32)


def rows_dot(a, b):
    return lax.dot_general(a, b, (((1,), (1,)), ((), ())), preferred_element_type=F32)


def two_parts(x):
    high = x.astype(BF16)
    low = (x - high.astype(F32)).astype(BF16)
    return jnp.concatenate([high, low], axis=0)


def exact_dot(x, b):
    both = wide_dot(two_parts(x), b)
    return both[:TOKENS] + both[TOKENS:]


def over_memory(x, combine):
    for shift in (64, 32, 16):
        x = combine(x, pltpu.roll(x, shift, axis=1))
    return x


def chain_kernel(h_ref, g_ref, kv_ref, out_ref, kd, vd, hs, gs, sc_s, p_s, ds_s, scale_s, turned):
    root = HEAD_DIMENSION**-0.5

    def spread(section):
        head_row = lax.broadcasted_iota(jnp.int32, (HEADS, 256), 0)
        lane_head = lax.broadcasted_iota(jnp.int32, (HEADS, 256), 1) >> 7
        for block in range(8):
            own = head_row == lane_head + 2 * block
            for offset, target in ((0, kd), (256, vd)):
                part = kv_ref[section, block, :, offset : offset + 256].astype(F32)
                for m in range(MEM):
                    row = jnp.broadcast_to(part[m : m + 1], (HEADS, 256))
                    target[section, m * HEADS : (m + 1) * HEADS, block * 256 : (block + 1) * 256] = (
                        jnp.where(own, row, 0.0).astype(BF16)
                    )

    spread(0)
    state = h_ref[...]
    for s in range(SECTIONS):
        wide = state.astype(F32)
        hs[s] = wide
        raw = rows_dot(state, kd[s])
        scale = lax.rsqrt(jnp.mean(wide * wide, axis=-1, keepdims=True) + 1e-06)
        scores = raw * (scale * root)
        e = jnp.exp(scores - over_memory(scores, jnp.maximum))
        p = e / over_memory(e, jnp.add)
        sc_s[s] = scores
        p_s[s] = p
        scale_s[s] = jnp.broadcast_to(scale, (TOKENS, LANES))
        if s + 1 < SECTIONS:
            spread(s + 1)
            state = (wide + exact_dot(p, vd[s])).astype(BF16)

    grad = g_ref[...]
    for s in reversed(range(SECTIONS)):
        wide = grad.astype(F32)
        gs[s] = wide
        p = p_s[s]
        dp = rows_dot(grad, vd[s])
        ds = p * (dp - over_memory(p * dp, jnp.add))
        scale = scale_s[s][:, :1]
        ds_s[s] = ds * (scale_s[s] * root)
        if s > 0:
            along = jnp.sum(ds * sc_s[s], axis=-1, keepdims=True) * (1.0 / WIDTH)
            du = exact_dot(ds * root, kd[s])
            grad = (wide + scale * (du - hs[s] * (scale * along))).astype(BF16)

    row_section = lax.broadcasted_iota(jnp.int32, (LANES, LANES), 0) >> 3
    lane_section = lax.broadcasted_iota(jnp.int32, (LANES, LANES), 1) >> 3
    same = row_section == lane_section
    for coefficients, factors, offset in ((ds_s, hs, 0), (p_s, gs, 256)):
        turned[...] = coefficients[...].reshape(SECTIONS * TOKENS, LANES).T
        for head in range(HEADS):
            mine = turned[pl.ds(head, MEM, stride=HEADS), :]
            spread_out = jnp.broadcast_to(mine[None], (SECTIONS, MEM, LANES)).reshape(LANES, LANES)
            left = jnp.where(same, spread_out, 0.0).astype(BF16)
            lanes = slice(head * 128, head * 128 + 128)
            right = factors[:, :, lanes].reshape(SECTIONS * TOKENS, 128).astype(BF16)
            result = wide_dot(left, right).astype(BF16).reshape(SECTIONS, MEM, 128)
            start = offset + (head % 2) * 128
            out_ref[:, head // 2, :, start : start + 128] = result


def chain(h, g, kv):
    vmem = pl.BlockSpec(memory_space=pltpu.VMEM)
    return pl.pallas_call(
        chain_kernel,
        out_shape=jax.ShapeDtypeStruct((SECTIONS, 8, MEM, 512), BF16),
        in_specs=[vmem] * 3,
        out_specs=vmem,
        scratch_shapes=[
            pltpu.VMEM((SECTIONS, LANES, WIDTH), BF16),
            pltpu.VMEM((SECTIONS, LANES, WIDTH), BF16),
            pltpu.VMEM((SECTIONS, TOKENS, WIDTH), F32),
            pltpu.VMEM((SECTIONS, TOKENS, WIDTH), F32),
            pltpu.VMEM((SECTIONS, TOKENS, LANES), F32),
            pltpu.VMEM((SECTIONS, TOKENS, LANES), F32),
            pltpu.VMEM((SECTIONS, TOKENS, LANES), F32),
            pltpu.VMEM((SECTIONS, TOKENS, LANES), F32),
            pltpu.VMEM((LANES, LANES), F32),
        ],
        compiler_params=pltpu.CompilerParams(vmem_limit_bytes=48 * 1024 * 1024),
        name="sections",
    )(h, g, kv)


def swap(block, axis):
    return lax.ppermute(block, axis, [(0, 1), (1, 0)])


def exchange(block, axes):
    return lax.all_to_all(block, axes, split_axis=0, concat_axis=0, tiled=True)


def in_order(blocks, zl, c):
    a, b, d, e = blocks
    a, b = jnp.where(c == 0, a, b), jnp.where(c == 0, b, a)
    d, e = jnp.where(c == 0, d, e), jnp.where(c == 0, e, d)
    low = zl == 0
    return [jnp.where(low, a, d), jnp.where(low, b, e), jnp.where(low, d, a), jnp.where(low, e, b)]


def owner_route():
    route = []
    for slot in range(128):
        for member in range(4):
            y, k = divmod(slot, 16)
            route.append((slot * 4 + member, (y * 4 + member) * 16 + k))
    return route


def body(memory, decoder_in, key_weight, value_weight, top_grad):
    place = lax.axis_index(SECTION)
    zl, c = lax.axis_index("zl"), lax.axis_index("c")

    own = jnp.concatenate([key_weight[0], value_weight[0]], axis=1)
    far = swap(own, "zl")
    weights = [own, swap(own, "c"), far, swap(far, "c")]

    piece = memory.reshape(1, 16, 128)
    every = exchange(jnp.broadcast_to(piece, (128, 16, 128)), RING)
    rows = every.reshape(16, 8, 16, 128).transpose(1, 2, 0, 3).reshape(128, 2048)
    parts = [jnp.dot(rows, w, preferred_element_type=F32).astype(BF16) for w in weights]
    parts = in_order(parts, zl, c)
    projected = jnp.concatenate([q[:, :64] for q in parts] + [q[:, 64:] for q in parts], axis=1)

    columns = exchange(projected.reshape(8, 16, 512), "y")
    columns = columns.reshape(8, 2, MEM, 512).transpose(1, 0, 2, 3)
    outgoing = jnp.broadcast_to(columns[:, None], (2, 8, 8, MEM, 512)).reshape(16, 8, MEM, 512)
    kv = exchange(outgoing, SECTION)

    start = (place % 8) * TOKENS
    mine = (place // 8, start, 0)
    h = lax.dynamic_slice(decoder_in, mine, (1, TOKENS, WIDTH))[0]
    g = lax.dynamic_slice(top_grad, mine, (1, TOKENS, WIDTH))[0]
    grads = chain(h, g, kv)

    shares = exchange(grads, SECTION).reshape(2, 8, 8, MEM, 512)
    summed = jnp.sum(shares.astype(F32), axis=1).astype(BF16)
    back = exchange(summed.transpose(1, 0, 2, 3), "y").reshape(128, 512)
    quarters = [
        jnp.concatenate([back[:, 64 * i : 64 * i + 64], back[:, 256 + 64 * i : 320 + 64 * i]], axis=1)
        for i in range(4)
    ]
    quarters = in_order(quarters, zl, c)
    term = sum(rows_dot(q, w) for q, w in zip(quarters, weights))
    pieces = exchange(term.astype(BF16).reshape(128, 1, 2048), RING)
    total = jnp.sum(pieces.astype(F32), axis=0)
    return lax.ppermute(total, RING + ("zl", "c"), owner_route())


def solution(mesh):
    fine = Mesh(mesh.devices.reshape(4, 4, 8, 2, 2), ("zh", "x", "y", "zl", "c"))
    placed = (
        P(DP, None, SECTION),
        P(DP, None, None),
        P(SECTION, None, DP),
        P(SECTION, None, DP),
        P(DP, None, None),
    )
    return jax.shard_map(
        body, mesh=fine, in_specs=placed, out_specs=P(SECTION + DP, None), check_vma=False
    )
```

time: 1050 us -> 213 us (0.20)
  waiting for transfers between devices: 684 us -> 45.5 us
  starting transfers between devices: 155 us -> 46.7 us
  matrix products: 71.9 us -> 2.4 us
  Pallas kernels: 0 us -> 26.6 us
  other arithmetic: 17.4 us -> 2.64 us
  between operations: 13.6 us -> 0.29 us
    unnamed x3 -> x0, waiting for transfers between devices: 313 us -> none
    ppermute x34 -> x4, waiting for transfers between devices: 292 us -> 19.6 us  [the longest x3 18.8 us: swap(): return lax.ppermute(block, axis, [(0, 1), (1, 0)])]
    ppermute x34 -> x4, starting transfers between devices: 148 us -> 16.9 us  [the longest x3 8.62 us: swap(): return lax.ppermute(block, axis, [(0, 1), (1, 0)])]
    all_gather x1 -> x0, waiting for transfers between devices: 69.7 us -> none  [body(): every = lax.all_gather(wide, 'dp', axis=0, tiled=True)]
    dot_general x121 -> x8, matrix products: 71.9 us -> 2.4 us  [the longest x4 1.25 us: body(): jnp.dot(rows, w, preferred_element_type=F32).astype(BF16)]
    all_gather x1 -> x0, blocking collectives: 45.8 us -> none  [body(): wide = lax.all_gather(memory, 'section', axis=2, tiled=True)]
    all_to_all x1 -> x4, blocking collectives: 42 us -> 79.6 us  [exchange(): return lax.all_to_all(block, axes, split_axis=0, concat_axis=0, tiled=True)]
    pallas_call x0 -> x1, Pallas kernels: none -> 26.6 us  [chain(): pl.pallas_call(chain_kernel, out_shape=jax.ShapeDtypeStruct((SECTIONS, 8,...]
  transfers between devices with their start and end apart: 37 -> 6, of which waited for: 37 -> 4; matrix products, arithmetic and copies ran while one was open for 2% -> 1% of each run, Pallas kernels for 0% -> 0%
where the time goes in v1:
time: 213 us; the launch traced here: 210 us
  blocking collectives  79.6 us (37%)
  starting transfers between devices  46.7 us (22%)
  waiting for transfers between devices  45.5 us (21%)
  Pallas kernels  26.6 us (12%)
  local copies, waits for them, and re-layouts  5.99 us (3%)
  other arithmetic  2.64 us (1%)
  matrix products  2.4 us (1%)
    all_to_all x4, blocking collectives, exchange(): return lax.all_to_all(block, axes, split_axis=0, concat_axis=0, tiled=True)  79.6 us
    all_to_all x2, starting transfers between devices, exchange(): return lax.all_to_all(block, axes, split_axis=0, concat_axis=0, tiled=True)  29.8 us
    pallas_call x1, Pallas kernels, chain(): pl.pallas_call(chain_kernel, out_shape=jax.ShapeDtypeStruct((SECTIONS, 8,...  26.6 us
    all_to_all x2, waiting for transfers between devices, exchange(): return lax.all_to_all(block, axes, split_axis=0, concat_axis=0, tiled=True)  26 us
    ppermute x3, waiting for transfers between devices, swap(): return lax.ppermute(block, axis, [(0, 1), (1, 0)])  18.8 us
    ppermute x3, starting transfers between devices, swap(): return lax.ppermute(block, axis, [(0, 1), (1, 0)])  8.62 us
    ppermute x1, starting transfers between devices, body(): return lax.ppermute(total, RING + ('zl', 'c'), owner_route())  8.23 us
  transfers between devices with their start and end apart: 6, of which 4 were waited for; matrix products, arithmetic and copies ran while one was open for 1% of the time, Pallas kernels for 0%

profile of v1, /device:TPU:1, one launch (start us, length us, event | category | flops | bytes accessed | tf_op | source)
XLA Modules:
  0.0 209.7 jit_solution(4066017599245381233)
XLA Ops:
  0.0 1.6 broadcast_in_dim.14
  1.6 0.0 copy-start
  1.6 0.0 copy-start.1
  1.6 20.9 %all-to-all-start = ((bf16[128,16,128]{2,1,0:T(8,128)(2,1)}), bf16[128,16,128]{2,1,0:T(8,128)(2,1)S(1)}, u32[]{:S(2)}, u32[]{:S(2)}) async-start(bf16[128,16,128]{2,1,0:T(8,128)(2,1)} %broadcast_in_dim.14), calls=%async_computation | async-start | bytes 1048576 | tf_op jit(solution)/shard_map/all_to_all | solution.py:141
  22.5 0.0 copy-done
  22.5 0.0 copy-done.1
  22.6 3.1 %collective-permute-start.1 = (bf16[2048,128]{0,1:T(8,128)(2,1)S(1)}, bf16[2048,128]{0,1:T(8,128)(2,1)S(1)}, u32[]{:S(2)}, u32[]{:S(2)}) collective-permute-start(bf16[2048,128]{0,1:T(8,128)(2,1)S(1)} %pad_maximum_fusion), channel_id=1, source_target_pairs={{0,2},{2,0},{1,3},{3,1},{4,6},{6,4},{5,7},{7,5},{8,10},{10,8},{9,1... | collective-permute-start | bytes 1572872 | tf_op jit(solution)/shard_map/ppermute | solution.py:137
  25.7 3.1 %collective-permute-start = (bf16[2048,128]{0,1:T(8,128)(2,1)S(1)}, bf16[2048,128]{0,1:T(8,128)(2,1)S(1)}, u32[]{:S(2)}, u32[]{:S(2)}) collective-permute-start(bf16[2048,128]{0,1:T(8,128)(2,1)S(1)} %pad_maximum_fusion), channel_id=1, source_target_pairs={{0,1},{1,0},{2,3},{3,2},{4,5},{5,4},{6,7},{7,6},{8,9},{9,8},{10,11... | collective-permute-start | bytes 1572872 | tf_op jit(solution)/shard_map/ppermute | solution.py:137
  28.8 18.6 %collective-permute-done.1 = bf16[2048,128]{0,1:T(8,128)(2,1)S(1)} collective-permute-done((bf16[2048,128]{0,1:T(8,128)(2,1)S(1)}, bf16[2048,128]{0,1:T(8,128)(2,1)S(1)}, u32[]{:S(2)}, u32[]{:S(2)}) %collective-permute-start.1) | collective-permute-done | bytes 524320 | tf_op jit(solution)/shard_map/ppermute | solution.py:137
  47.4 2.4 %collective-permute-start.2 = (bf16[2048,128]{0,1:T(8,128)(2,1)S(1)}, bf16[2048,128]{0,1:T(8,128)(2,1)S(1)}, u32[]{:S(2)}, u32[]{:S(2)}) collective-permute-start(bf16[2048,128]{0,1:T(8,128)(2,1)S(1)} %collective-permute-done.1), channel_id=1, source_target_pairs={{0,1},{1,0},{2,3},{3,2},{4,5},{5,4},{6,7},{7,6},{8,9},{9,8},{10,11... | collective-permute-start | bytes 1572872 | tf_op jit(solution)/shard_map/ppermute | solution.py:137
  49.8 0.0 all-to-all-done
  49.8 0.3 copy.17
  50.2 0.3 convolution_convert_fusion.3
  50.5 0.3 convolution_convert_fusion.1
  50.8 0.0 collective-permute-done
  50.8 0.3 convolution_convert_fusion.2
  51.2 0.2 collective-permute-done.2
  51.3 0.3 select_bitcast_fusion
  51.8 0.1 copy.18
  51.9 12.8 %all_to_all.30 = bf16[8,16,512]{2,1,0:T(8,128)(2,1)S(1)} all-to-all(bf16[8,16,512]{2,1,0:T(8,128)(2,1)S(1)} %bitcast.62), channel_id=1, replica_groups=mesh['zh'=4,'x'=4,'y'=8,'zl'=2,'c'=2] {'y'}, dimensions={0} | all-to-all | bytes 262144 | tf_op jit(solution)/shard_map/all_to_all | solution.py:141
  64.7 1.1 broadcast_in_dim.15
  65.8 8.9 %all-to-all-start.2 = ((bf16[16,8,8,512]{3,2,1,0:T(8,128)(2,1)}), bf16[16,8,8,512]{3,2,1,0:T(8,128)(2,1)S(1)}, u32[]{:S(2)}, u32[]{:S(2)}) async-start(bf16[16,8,8,512]{3,2,1,0:T(8,128)(2,1)} %bitcast.14), calls=%async_computation.2 | async-start | bytes 2097152 | tf_op jit(solution)/shard_map/all_to_all | solution.py:141
  74.7 0.8 dynamic-slice_bitcast_fusion
  75.5 26.0 %all-to-all-done.2.kv_ref = bf16[16,8,8,512]{3,2,1,0:T(8,128)(2,1)S(1)} async-done(((bf16[16,8,8,512]{3,2,1,0:T(8,128)(2,1)}), bf16[16,8,8,512]{3,2,1,0:T(8,128)(2,1)S(1)}, u32[]{:S(2)}, u32[]{:S(2)}) %all-to-all-start.2) | async-done | bytes 1048608 | tf_op jit(solution)/shard_map/all_to_all | solution.py:141
  101.4 26.6 %sections.1 = bf16[16,8,8,512]{3,2,1,0:T(8,128)(2,1)S(1)} custom-call(bf16[8,2048]{1,0:T(8,128)(2,1)S(1)} %get-tuple-element.18.h_ref, bf16[8,2048]{1,0:T(8,128)(2,1)S(1)} %get-tuple-element.17.g_ref, bf16[16,8,8,512]{3,2,1,0:T(8,128)(2,1)S(1)} %all-to-all-done.2.kv_ref), custom_call_target="tpu_custom_call" | custom-call | tf_op jit(solution)/shard_map/sections/pallas_call | solution.py:115
  128.0 29.5 %all_to_all.31 = bf16[16,8,8,512]{3,2,1,0:T(8,128)(2,1)S(1)} all-to-all(bf16[16,8,8,512]{3,2,1,0:T(8,128)(2,1)S(1)} %sections.1), channel_id=1, replica_groups=mesh['zh'=4,'x'=4,'y'=8,'zl'=2,'c'=2] {'zh','x'}, dimensions={0} | all-to-all | bytes 2097152 | tf_op jit(solution)/shard_map/all_to_all | solution.py:141
  157.6 0.1 bitcast_reduce_fusion
  157.7 11.9 %all_to_all.32 = bf16[8,2,8,512]{3,2,1,0:T(8,128)(2,1)S(1)} all-to-all(bf16[8,2,8,512]{3,2,1,0:T(8,128)(2,1)S(1)} %copy.20), channel_id=1, replica_groups=mesh['zh'=4,'x'=4,'y'=8,'zl'=2,'c'=2] {'y'}, dimensions={0} | all-to-all | bytes 262144 | tf_op jit(solution)/shard_map/all_to_all | solution.py:141
  169.6 0.1 fusion.19
  169.7 0.1 pad_maximum_fusion.4
  169.8 0.1 pad_maximum_fusion.3
  169.9 0.1 pad_maximum_fusion.2
  170.0 0.1 pad_maximum_fusion.1
  170.0 0.3 fusion.13
  170.3 0.3 convolution_add_fusion.2
  170.6 0.3 convolution_add_fusion.1
  170.9 0.3 fusion.1
  171.2 0.5 broadcast.13
  171.7 1.0 reduce.2
  172.7 0.4 reshape.36
  173.1 25.4 %all_to_all.33 = bf16[128,2,1024]{2,1,0:T(2,128)(2,1)S(1)} all-to-all(bf16[128,2,1024]{2,1,0:T(2,128)(2,1)S(1)} %reshape.36), channel_id=1, replica_groups=mesh['zh'=4,'x'=4,'y'=8,'zl'=2,'c'=2] {'zh','x','y'}, dimensions={0} | all-to-all | bytes 1048576 | tf_op jit(solution)/shard_map/all_to_all | solution.py:141
  198.5 0.4 reshape.37
  198.9 1.1 convert_reduce_fusion
  200.1 8.2 %collective-permute-start.3 = (f32[1,2048]{1,0:T(1,128)S(1)}, f32[1,2048]{1,0:T(1,128)S(1)}, u32[]{:S(2)}, u32[]{:S(2)}) collective-permute-start(f32[1,2048]{1,0:T(1,128)S(1)} %bitcast.64), channel_id=1, source_target_pairs={{0,0},{1,16},{2,32},{3,48},{4,1},{5,17},{6,33},{7,49},{8,2},{9,18}... | collective-permute-start | bytes 24584 | tf_op jit(solution)/shard_map/ppermute | solution.py:198
  208.3 0.8 collective-permute-done.3
  209.1 0.6 copy.50
  (11 shorter events, 0.1 us)
Async XLA Ops:
  1.6 21.0 %copy-start = (bf16[1,2048,64]{1,2,0:T(8,128)(2,1)S(1)}, bf16[1,2048,64]{1,2,0:T(8,128)(2,1)}, u32[]{:S(2)}) copy-start(bf16[1,2048,64]{1,2,0:T(8,128)(2,1)} %param.8) | copy-start | bytes 786436
  1.6 21.0 %copy-start.1 = (bf16[1,2048,64]{1,2,0:T(8,128)(2,1)S(1)}, bf16[1,2048,64]{1,2,0:T(8,128)(2,1)}, u32[]{:S(2)}) copy-start(bf16[1,2048,64]{1,2,0:T(8,128)(2,1)} %param.7) | copy-start | bytes 786436
  1.6 48.3 %all-to-all-start = ((bf16[128,16,128]{2,1,0:T(8,128)(2,1)}), bf16[128,16,128]{2,1,0:T(8,128)(2,1)S(1)}, u32[]{:S(2)}, u32[]{:S(2)}) async-start(bf16[128,16,128]{2,1,0:T(8,128)(2,1)} %broadcast_in_dim.14), calls=%async_computation | async-start | bytes 1048576 | tf_op jit(solution)/shard_map/all_to_all | solution.py:141
  22.6 24.9 %collective-permute-start.1 = (bf16[2048,128]{0,1:T(8,128)(2,1)S(1)}, bf16[2048,128]{0,1:T(8,128)(2,1)S(1)}, u32[]{:S(2)}, u32[]{:S(2)}) collective-permute-start(bf16[2048,128]{0,1:T(8,128)(2,1)S(1)} %pad_maximum_fusion), channel_id=1, source_target_pairs={{0,2},{2,0},{1,3},{3,1},{4,6},{6,4},{5,7},{7,5},{8,10},{10,8},{9,1... | collective-permute-start | bytes 1572872 | tf_op jit(solution)/shard_map/ppermute | solution.py:137
  25.7 25.2 %collective-permute-start = (bf16[2048,128]{0,1:T(8,128)(2,1)S(1)}, bf16[2048,128]{0,1:T(8,128)(2,1)S(1)}, u32[]{:S(2)}, u32[]{:S(2)}) collective-permute-start(bf16[2048,128]{0,1:T(8,128)(2,1)S(1)} %pad_maximum_fusion), channel_id=1, source_target_pairs={{0,1},{1,0},{2,3},{3,2},{4,5},{5,4},{6,7},{7,6},{8,9},{9,8},{10,11... | collective-permute-start | bytes 1572872 | tf_op jit(solution)/shard_map/ppermute | solution.py:137
  47.4 3.9 %collective-permute-start.2 = (bf16[2048,128]{0,1:T(8,128)(2,1)S(1)}, bf16[2048,128]{0,1:T(8,128)(2,1)S(1)}, u32[]{:S(2)}, u32[]{:S(2)}) collective-permute-start(bf16[2048,128]{0,1:T(8,128)(2,1)S(1)} %collective-permute-done.1), channel_id=1, source_target_pairs={{0,1},{1,0},{2,3},{3,2},{4,5},{5,4},{6,7},{7,6},{8,9},{9,8},{10,11... | collective-permute-start | bytes 1572872 | tf_op jit(solution)/shard_map/ppermute | solution.py:137
  65.8 35.7 %all-to-all-start.2 = ((bf16[16,8,8,512]{3,2,1,0:T(8,128)(2,1)}), bf16[16,8,8,512]{3,2,1,0:T(8,128)(2,1)S(1)}, u32[]{:S(2)}, u32[]{:S(2)}) async-start(bf16[16,8,8,512]{3,2,1,0:T(8,128)(2,1)} %bitcast.14), calls=%async_computation.2 | async-start | bytes 2097152 | tf_op jit(solution)/shard_map/all_to_all | solution.py:141
  200.1 9.0 %collective-permute-start.3 = (f32[1,2048]{1,0:T(1,128)S(1)}, f32[1,2048]{1,0:T(1,128)S(1)}, u32[]{:S(2)}, u32[]{:S(2)}) collective-permute-start(f32[1,2048]{1,0:T(1,128)S(1)} %bitcast.64), channel_id=1, source_target_pairs={{0,0},{1,16},{2,32},{3,48},{4,1},{5,17},{6,33},{7,49},{8,2},{9,18}... | collective-permute-start | bytes 24584 | tf_op jit(solution)/shard_map/ppermute | solution.py:198

commit v2 on v1

--- a/solution.py
+++ b/solution.py
@@ -1,5 +1,3 @@
-import functools
-
 import jax
 import jax.numpy as jnp
 from jax import lax
@@ -18,6 +16,7 @@
 SECTION = ("zh", "x")
 DP = ("y", "zl", "c")
 RING = ("zh", "x", "y")
+MEM_ORDER = [4 * m2 + 2 * zl + c for zl in range(2) for c in range(2) for m2 in range(2)]
 F32 = jnp.float32
 BF16 = jnp.bfloat16
 
@@ -45,6 +44,10 @@
     for shift in (64, 32, 16):
         x = combine(x, pltpu.roll(x, shift, axis=1))
     return x
+
+
+def slot(section):
+    return section % 4 * 4 + section // 4
 
 
 def chain_kernel(h_ref, g_ref, kv_ref, out_ref, kd, vd, hs, gs, sc_s, p_s, ds_s, scale_s, turned):
@@ -56,10 +59,10 @@
         for block in range(8):
             own = head_row == lane_head + 2 * block
             for offset, target in ((0, kd), (256, vd)):
-                part = kv_ref[section, block, :, offset : offset + 256].astype(F32)
-                for m in range(MEM):
+                part = kv_ref[slot(section), block, :, offset : offset + 256].astype(F32)
+                for i, m in enumerate(MEM_ORDER):
                     row = jnp.broadcast_to(part[m : m + 1], (HEADS, 256))
-                    target[section, m * HEADS : (m + 1) * HEADS, block * 256 : (block + 1) * 256] = (
+                    target[section, i * HEADS : (i + 1) * HEADS, block * 256 : (block + 1) * 256] = (
                         jnp.where(own, row, 0.0).astype(BF16)
                     )
 
@@ -107,7 +110,8 @@
             right = factors[:, :, lanes].reshape(SECTIONS * TOKENS, 128).astype(BF16)
             result = wide_dot(left, right).astype(BF16).reshape(SECTIONS, MEM, 128)
             start = offset + (head % 2) * 128
-            out_ref[:, head // 2, :, start : start + 128] = result
+            for s in range(SECTIONS):
+                out_ref[slot(s), head // 2, :, start : start + 128] = result[s]
 
 
 def chain(h, g, kv):
@@ -149,44 +153,42 @@
     return [jnp.where(low, a, d), jnp.where(low, b, e), jnp.where(low, d, a), jnp.where(low, e, b)]
 
 
-def owner_route():
-    route = []
-    for slot in range(128):
-        for member in range(4):
-            y, k = divmod(slot, 16)
-            route.append((slot * 4 + member, (y * 4 + member) * 16 + k))
-    return route
-
-
 def body(memory, decoder_in, key_weight, value_weight, top_grad):
-    place = lax.axis_index(SECTION)
+    zh, x = lax.axis_index("zh"), lax.axis_index("x")
     zl, c = lax.axis_index("zl"), lax.axis_index("c")
 
     own = jnp.concatenate([key_weight[0], value_weight[0]], axis=1)
+    near = swap(own, "c")
     far = swap(own, "zl")
-    weights = [own, swap(own, "c"), far, swap(far, "c")]
-
-    piece = memory.reshape(1, 16, 128)
+    weights = [own, near, far, swap(far, "c")]
+
+    piece, near = lax.optimization_barrier((memory.reshape(1, 16, 128), near))
     every = exchange(jnp.broadcast_to(piece, (128, 16, 128)), RING)
     rows = every.reshape(16, 8, 16, 128).transpose(1, 2, 0, 3).reshape(128, 2048)
     parts = [jnp.dot(rows, w, preferred_element_type=F32).astype(BF16) for w in weights]
     parts = in_order(parts, zl, c)
     projected = jnp.concatenate([q[:, :64] for q in parts] + [q[:, 64:] for q in parts], axis=1)
 
-    columns = exchange(projected.reshape(8, 16, 512), "y")
-    columns = columns.reshape(8, 2, MEM, 512).transpose(1, 0, 2, 3)
-    outgoing = jnp.broadcast_to(columns[:, None], (2, 8, 8, MEM, 512)).reshape(16, 8, MEM, 512)
-    kv = exchange(outgoing, SECTION)
-
-    start = (place % 8) * TOKENS
-    mine = (place // 8, start, 0)
+    columns = projected.reshape(8, 2, MEM, 512).transpose(1, 0, 2, 3)
+    outgoing = jnp.broadcast_to(columns[:, None], (2, 2, 8, MEM, 512)).reshape(32, MEM, 512)
+    held = exchange(outgoing, ("zh", "y")).reshape(1, 4, 8, MEM, 512)
+    kv = exchange(jnp.broadcast_to(held, (4, 4, 8, MEM, 512)), "x").reshape(16, 8, MEM, 512)
+
+    mine = (zh // 2, (zh % 2 * 4 + x) * TOKENS, 0)
     h = lax.dynamic_slice(decoder_in, mine, (1, TOKENS, WIDTH))[0]
     g = lax.dynamic_slice(top_grad, mine, (1, TOKENS, WIDTH))[0]
     grads = chain(h, g, kv)
 
-    shares = exchange(grads, SECTION).reshape(2, 8, 8, MEM, 512)
-    summed = jnp.sum(shares.astype(F32), axis=1).astype(BF16)
-    back = exchange(summed.transpose(1, 0, 2, 3), "y").reshape(128, 512)
+    shares = exchange(grads.reshape(4, 4, 8, MEM, 512), "x")
+    summed = jnp.sum(shares.astype(F32), axis=0).astype(BF16)
+    halves = exchange(summed.reshape(64, 4, 512), ("zh", "y", "zl"))
+    halves = halves.reshape(2, 2, 8, 2, 2, 2, 512).astype(F32)
+    summed = jnp.sum(halves, axis=1).astype(BF16)
+    kept = jnp.where(c == 0, summed[:, :, :, 0], summed[:, :, :, 1])
+    given = jnp.where(c == 0, summed[:, :, :, 1], summed[:, :, :, 0])
+    got = swap(given, "c")
+    first, second = jnp.where(c == 0, kept, got), jnp.where(c == 0, got, kept)
+    back = jnp.stack([first, second]).transpose(2, 3, 0, 1, 4, 5).reshape(128, 512)
     quarters = [
         jnp.concatenate([back[:, 64 * i : 64 * i + 64], back[:, 256 + 64 * i : 320 + 64 * i]], axis=1)
         for i in range(4)
@@ -194,8 +196,7 @@
     quarters = in_order(quarters, zl, c)
     term = sum(rows_dot(q, w) for q, w in zip(quarters, weights))
     pieces = exchange(term.astype(BF16).reshape(128, 1, 2048), RING)
-    total = jnp.sum(pieces.astype(F32), axis=0)
-    return lax.ppermute(total, RING + ("zl", "c"), owner_route())
+    return jnp.sum(pieces.astype(F32), axis=0)
 
 
 def solution(mesh):

time: 213 us -> 201 us (0.944); the launches traced: 210 us -> 200 us
  waiting for transfers between devices: 45.5 us -> 35.2 us
  starting transfers between devices: 46.7 us -> 40 us
  blocking collectives: 79.6 us -> 84.4 us
    all_to_all x2, waiting for transfers between devices: 26 us -> 11.4 us  [exchange(): return lax.all_to_all(block, axes, split_axis=0, concat_axis=0, tiled=True)]
    ppermute x3 -> x4, starting transfers between devices: 8.62 us -> 21.3 us  [swap(): return lax.ppermute(block, axis, [(0, 1), (1, 0)])]
    all_to_all x2, starting transfers between devices: 29.8 us -> 18.7 us  [exchange(): return lax.all_to_all(block, axes, split_axis=0, concat_axis=0, tiled=True)]
    ppermute x1 -> x0, starting transfers between devices: 8.23 us -> none  [body(): return lax.ppermute(total, RING + ('zl', 'c'), owner_route())]
    ppermute x3 -> x4, waiting for transfers between devices: 18.8 us -> 23.8 us  [swap(): return lax.ppermute(block, axis, [(0, 1), (1, 0)])]
    all_to_all x4, blocking collectives: 79.6 us -> 84.4 us  [exchange(): return lax.all_to_all(block, axes, split_axis=0, concat_axis=0, tiled=True)]
where the time goes in v2:
time: 201 us; the launch traced here: 200 us
  blocking collectives  84.4 us (42%)
  starting transfers between devices  40 us (20%)
  waiting for transfers between devices  35.2 us (18%)
  Pallas kernels  26.6 us (13%)
  local copies, waits for them, and re-layouts  6.55 us (3%)
  other arithmetic  4.45 us (2%)
  matrix products  2.57 us (1%)
    all_to_all x4, blocking collectives, exchange(): return lax.all_to_all(block, axes, split_axis=0, concat_axis=0, tiled=True)  84.4 us
    pallas_call x1, Pallas kernels, chain(): pl.pallas_call(chain_kernel, out_shape=jax.ShapeDtypeStruct((SECTIONS, 8,...  26.6 us
    ppermute x4, waiting for transfers between devices, swap(): return lax.ppermute(block, axis, [(0, 1), (1, 0)])  23.8 us
    ppermute x4, starting transfers between devices, swap(): return lax.ppermute(block, axis, [(0, 1), (1, 0)])  21.3 us
    all_to_all x2, starting transfers between devices, exchange(): return lax.all_to_all(block, axes, split_axis=0, concat_axis=0, tiled=True)  18.7 us
    all_to_all x2, waiting for transfers between devices, exchange(): return lax.all_to_all(block, axes, split_axis=0, concat_axis=0, tiled=True)  11.4 us
  transfers between devices with their start and end apart: 6, of which 4 were waited for; matrix products, arithmetic and copies ran while one was open for 1% of the time, Pallas kernels for 0%

profile of v2, /device:TPU:1, one launch (start us, length us, event | category | flops | bytes accessed | tf_op | source)
XLA Modules:
  0.0 200.1 jit_solution(11876226809739654650)
XLA Ops:
  0.0 0.0 copy-start.2
  0.0 1.1 pad_maximum_fusion
  1.1 8.8 %collective-permute-start = (bf16[2048,128]{0,1:T(8,128)(2,1)S(1)}, bf16[2048,128]{0,1:T(8,128)(2,1)S(1)}, u32[]{:S(2)}, u32[]{:S(2)}) collective-permute-start(bf16[2048,128]{0,1:T(8,128)(2,1)S(1)} %pad_maximum_fusion), channel_id=1, source_target_pairs={{0,1},{1,0},{2,3},{3,2},{4,5},{5,4},{6,7},{7,6},{8,9},{9,8},{10,11... | collective-permute-start | bytes 1572872 | tf_op jit(solution)/shard_map/ppermute | solution.py:141
  9.9 1.5 collective-permute-done
  11.4 0.0 copy-done.2
  11.4 0.9 broadcast_in_dim.21
  12.3 14.6 %all-to-all-start = ((bf16[128,16,128]{2,1,0:T(8,128)(2,1)}), bf16[128,16,128]{2,1,0:T(8,128)(2,1)S(1)}, u32[]{:S(2)}, u32[]{:S(2)}) async-start(bf16[128,16,128]{2,1,0:T(8,128)(2,1)} %broadcast_in_dim.21), calls=%async_computation | async-start | bytes 1048576 | tf_op jit(solution)/shard_map/all_to_all | solution.py:145
  26.9 3.1 %collective-permute-start.1 = (bf16[2048,128]{0,1:T(8,128)(2,1)S(1)}, bf16[2048,128]{0,1:T(8,128)(2,1)S(1)}, u32[]{:S(2)}, u32[]{:S(2)}) collective-permute-start(bf16[2048,128]{0,1:T(8,128)(2,1)S(1)} %pad_maximum_fusion), channel_id=1, source_target_pairs={{0,2},{2,0},{1,3},{3,1},{4,6},{6,4},{5,7},{7,5},{8,10},{10,8},{9,1... | collective-permute-start | bytes 1572872 | tf_op jit(solution)/shard_map/ppermute | solution.py:141
  30.0 21.6 %collective-permute-done.1 = bf16[2048,128]{0,1:T(8,128)(2,1)S(1)} collective-permute-done((bf16[2048,128]{0,1:T(8,128)(2,1)S(1)}, bf16[2048,128]{0,1:T(8,128)(2,1)S(1)}, u32[]{:S(2)}, u32[]{:S(2)}) %collective-permute-start.1) | collective-permute-done | bytes 524320 | tf_op jit(solution)/shard_map/ppermute | solution.py:141
  51.6 2.5 %collective-permute-start.2 = (bf16[2048,128]{0,1:T(8,128)(2,1)S(1)}, bf16[2048,128]{0,1:T(8,128)(2,1)S(1)}, u32[]{:S(2)}, u32[]{:S(2)}) collective-permute-start(bf16[2048,128]{0,1:T(8,128)(2,1)S(1)} %collective-permute-done.1), channel_id=1, source_target_pairs={{0,1},{1,0},{2,3},{3,2},{4,5},{5,4},{6,7},{7,6},{8,9},{9,8},{10,11... | collective-permute-start | bytes 1572872 | tf_op jit(solution)/shard_map/ppermute | solution.py:141
  54.1 0.0 all-to-all-done
  54.1 0.0 copy-start
  54.1 0.0 copy-start.1
  54.1 0.3 copy.79
  54.5 0.6 copy-done
  55.1 0.1 copy-done.1
  55.2 0.3 convolution_convert_fusion.3
  55.5 0.3 convolution_convert_fusion.1
  55.8 0.3 convolution_convert_fusion.2
  56.1 0.0 collective-permute-done.2
  56.1 0.3 broadcast_select_fusion.8
  56.5 0.1 copy.80
  56.7 22.8 %all_to_all.30 = bf16[32,8,512]{2,1,0:T(8,128)(2,1)S(1)} all-to-all(bf16[32,8,512]{2,1,0:T(8,128)(2,1)S(1)} %bitcast.80), channel_id=1, replica_groups=mesh['zh'=4,'x'=4,'y'=8,'zl'=2,'c'=2] {'zh','y'}, dimensions={0} | all-to-all | bytes 524288 | tf_op jit(solution)/shard_map/all_to_all | solution.py:145
  79.5 1.1 broadcast_in_dim.24
  80.6 4.1 %all-to-all-start.2 = ((bf16[4,4,8,8,512]{4,3,2,1,0:T(8,128)(2,1)}), bf16[4,4,8,8,512]{4,3,2,1,0:T(8,128)(2,1)S(1)}, u32[]{:S(2)}, u32[]{:S(2)}) async-start(bf16[4,4,8,8,512]{4,3,2,1,0:T(8,128)(2,1)} %broadcast_in_dim.24), calls=%async_computation.2 | async-start | bytes 2097152 | tf_op jit(solution)/shard_map/all_to_all | solution.py:145
  84.7 0.8 dynamic-slice_bitcast_fusion
  85.5 11.4 %all-to-all-done.2 = bf16[4,4,8,8,512]{4,3,2,1,0:T(8,128)(2,1)S(1)} async-done(((bf16[4,4,8,8,512]{4,3,2,1,0:T(8,128)(2,1)}), bf16[4,4,8,8,512]{4,3,2,1,0:T(8,128)(2,1)S(1)}, u32[]{:S(2)}, u32[]{:S(2)}) %all-to-all-start.2) | async-done | bytes 1048608 | tf_op jit(solution)/shard_map/all_to_all | solution.py:145
  96.9 26.6 %sections.1 = bf16[16,8,8,512]{3,2,1,0:T(8,128)(2,1)S(1)} custom-call(bf16[8,2048]{1,0:T(8,128)(2,1)S(1)} %get-tuple-element.24.h_ref, bf16[8,2048]{1,0:T(8,128)(2,1)S(1)} %get-tuple-element.23.g_ref, bf16[16,8,8,512]{3,2,1,0:T(8,128)(2,1)S(1)} %bitcast.76), custom_call_target="tpu_custom_call" | custom-call | tf_op jit(solution)/shard_map/sections/pallas_call | solution.py:119
  123.5 13.7 %all_to_all.31 = bf16[4,4,8,8,512]{4,3,2,1,0:T(8,128)(2,1)S(1)} all-to-all(bf16[4,4,8,8,512]{4,3,2,1,0:T(8,128)(2,1)S(1)} %bitcast.77), channel_id=1, replica_groups=mesh['zh'=4,'x'=4,'y'=8,'zl'=2,'c'=2] {'x'}, dimensions={0} | all-to-all | bytes 2097152 | tf_op jit(solution)/shard_map/all_to_all | solution.py:145
  137.2 0.2 reduce_sum.35
  137.4 0.1 reshape.48
  137.5 21.3 %all_to_all.32 = bf16[64,4,512]{2,1,0:T(4,128)(2,1)S(1)} all-to-all(bf16[64,4,512]{2,1,0:T(4,128)(2,1)S(1)} %reshape.48), channel_id=1, replica_groups=mesh['zh'=4,'x'=4,'y'=8,'zl'=2,'c'=2] {'zh','y','zl'}, dimensions={0} | all-to-all | bytes 524288 | tf_op jit(solution)/shard_map/all_to_all | solution.py:145
  158.8 0.1 reshape.52
  158.9 0.5 reduce_sum.36
  159.4 0.1 fusion.22
  159.5 6.9 %collective-permute-start.3 = (bf16[2,8,2,2,512]{4,1,3,2,0:T(8,128)(2,1)S(1)}, bf16[2,8,2,2,512]{4,1,3,2,0:T(8,128)(2,1)S(1)}, u32[]{:S(2)}, u32[]{:S(2)}) collective-permute-start(bf16[2,8,2,2,512]{4,1,3,2,0:T(8,128)(2,1)S(1)} %fusion.10), channel_id=1, source_target_pairs={{0,1},{1,0},{2,3},{3,2},{4,5},{5,4},{6,7},{7,6},{8,9},{9,8},{10,11... | collective-permute-start | bytes 196616 | tf_op jit(solution)/shard_map/ppermute | solution.py:141
  166.4 0.7 collective-permute-done.3
  167.1 0.1 copy.88
  167.3 0.1 reshape.50
  167.3 0.1 fusion.21
  167.4 0.1 copy.102
  167.5 0.1 copy.103
  167.6 0.1 copy.104
  167.7 0.1 copy.105
  167.8 0.1 copy.106
  167.9 0.1 copy.107
  168.0 0.1 copy.108
  168.1 0.1 copy.109
  168.2 0.3 fusion.15
  168.6 0.3 convolution_add_fusion.2
  168.9 0.3 convolution_add_fusion.1
  169.2 0.3 fusion.1
  169.6 0.5 broadcast.6
  170.1 1.0 reduce.3
  171.1 0.4 reshape.53
  171.5 26.6 %all_to_all.33 = bf16[128,2,1024]{2,1,0:T(2,128)(2,1)S(1)} all-to-all(bf16[128,2,1024]{2,1,0:T(2,128)(2,1)S(1)} %reshape.53), channel_id=1, replica_groups=mesh['zh'=4,'x'=4,'y'=8,'zl'=2,'c'=2] {'zh','x','y'}, dimensions={0} | all-to-all | bytes 1048576 | tf_op jit(solution)/shard_map/all_to_all | solution.py:145
  198.1 0.4 reshape.54
  198.5 1.6 convert_reduce_fusion
  (13 shorter events, 0.2 us)
Async XLA Ops:
  0.0 11.4 %copy-start.2 = (bf16[2,8,128]{2,1,0:T(8,128)(2,1)S(1)}, bf16[2,8,128]{2,1,0:T(8,128)(2,1)}, u32[]{:S(2)}) copy-start(bf16[2,8,128]{2,1,0:T(8,128)(2,1)} %param.5) | copy-start | bytes 12292
  1.1 10.3 %collective-permute-start = (bf16[2048,128]{0,1:T(8,128)(2,1)S(1)}, bf16[2048,128]{0,1:T(8,128)(2,1)S(1)}, u32[]{:S(2)}, u32[]{:S(2)}) collective-permute-start(bf16[2048,128]{0,1:T(8,128)(2,1)S(1)} %pad_maximum_fusion), channel_id=1, source_target_pairs={{0,1},{1,0},{2,3},{3,2},{4,5},{5,4},{6,7},{7,6},{8,9},{9,8},{10,11... | collective-permute-start | bytes 1572872 | tf_op jit(solution)/shard_map/ppermute | solution.py:141
  12.3 41.8 %all-to-all-start = ((bf16[128,16,128]{2,1,0:T(8,128)(2,1)}), bf16[128,16,128]{2,1,0:T(8,128)(2,1)S(1)}, u32[]{:S(2)}, u32[]{:S(2)}) async-start(bf16[128,16,128]{2,1,0:T(8,128)(2,1)} %broadcast_in_dim.21), calls=%async_computation | async-start | bytes 1048576 | tf_op jit(solution)/shard_map/all_to_all | solution.py:145
  26.9 24.7 %collective-permute-start.1 = (bf16[2048,128]{0,1:T(8,128)(2,1)S(1)}, bf16[2048,128]{0,1:T(8,128)(2,1)S(1)}, u32[]{:S(2)}, u32[]{:S(2)}) collective-permute-start(bf16[2048,128]{0,1:T(8,128)(2,1)S(1)} %pad_maximum_fusion), channel_id=1, source_target_pairs={{0,2},{2,0},{1,3},{3,1},{4,6},{6,4},{5,7},{7,5},{8,10},{10,8},{9,1... | collective-permute-start | bytes 1572872 | tf_op jit(solution)/shard_map/ppermute | solution.py:141
  51.6 4.5 %collective-permute-start.2 = (bf16[2048,128]{0,1:T(8,128)(2,1)S(1)}, bf16[2048,128]{0,1:T(8,128)(2,1)S(1)}, u32[]{:S(2)}, u32[]{:S(2)}) collective-permute-start(bf16[2048,128]{0,1:T(8,128)(2,1)S(1)} %collective-permute-done.1), channel_id=1, source_target_pairs={{0,1},{1,0},{2,3},{3,2},{4,5},{5,4},{6,7},{7,6},{8,9},{9,8},{10,11... | collective-permute-start | bytes 1572872 | tf_op jit(solution)/shard_map/ppermute | solution.py:141
  54.1 1.0 copy-start
  54.1 1.0 copy-start.1
  80.6 16.3 %all-to-all-start.2 = ((bf16[4,4,8,8,512]{4,3,2,1,0:T(8,128)(2,1)}), bf16[4,4,8,8,512]{4,3,2,1,0:T(8,128)(2,1)S(1)}, u32[]{:S(2)}, u32[]{:S(2)}) async-start(bf16[4,4,8,8,512]{4,3,2,1,0:T(8,128)(2,1)} %broadcast_in_dim.24), calls=%async_computation.2 | async-start | bytes 2097152 | tf_op jit(solution)/shard_map/all_to_all | solution.py:145
  159.5 7.6 %collective-permute-start.3 = (bf16[2,8,2,2,512]{4,1,3,2,0:T(8,128)(2,1)S(1)}, bf16[2,8,2,2,512]{4,1,3,2,0:T(8,128)(2,1)S(1)}, u32[]{:S(2)}, u32[]{:S(2)}) collective-permute-start(bf16[2,8,2,2,512]{4,1,3,2,0:T(8,128)(2,1)S(1)} %fusion.10), channel_id=1, source_target_pairs={{0,1},{1,0},{2,3},{3,2},{4,5},{5,4},{6,7},{7,6},{8,9},{9,8},{10,11... | collective-permute-start | bytes 196616 | tf_op jit(solution)/shard_map/ppermute | solution.py:141

commit v3 on v2

v3 whole, which is shorter than its diff:
```python
import jax
import jax.numpy as jnp
from jax import lax
from jax.experimental import pallas as pl
from jax.experimental.pallas import tpu as pltpu
from jax.sharding import Mesh
from jax.sharding import PartitionSpec as P

HEADS = 16
HEAD_DIMENSION = 128
SECTIONS = 16
MEM = 8
TOKENS = 8
WIDTH = HEADS * HEAD_DIMENSION
LANES = MEM * HEADS
SECTION = ("zh", "x")
DP = ("yh", "yl", "zl", "c")
BLOCK = ("yh", "zl")
RING = SECTION + BLOCK
F32 = jnp.float32
BF16 = jnp.bfloat16


def wide_dot(a, b):
    return lax.dot_general(a, b, (((1,), (0,)), ((), ())), preferred_element_type=F32)


def rows_dot(a, b):
    return lax.dot_general(a, b, (((1,), (1,)), ((), ())), preferred_element_type=F32)


def two_parts(x):
    high = x.astype(BF16)
    low = (x - high.astype(F32)).astype(BF16)
    return jnp.concatenate([high, low], axis=0)


def exact_dot(x, b):
    both = wide_dot(two_parts(x), b)
    return both[:TOKENS] + both[TOKENS:]


def others(x):
    return [pltpu.roll(x, k * HEADS, axis=1) for k in range(1, MEM)]


def tree(terms):
    while len(terms) > 1:
        terms = [a + b for a, b in zip(terms[::2], terms[1::2])] + terms[len(terms) // 2 * 2 :]
    return terms[0]


def slot(section):
    return section % 4 * 4 + section // 4


def head_place(head):
    yh, yl, zl = head // 4, head // 2 % 2, head % 2
    return yh * 2 + zl, yl * 128


def chain_kernel(h_ref, g_ref, kv_ref, out_ref, left, right, key_rows, value_rows, hs, gs, sc_s, p_s, ds_s, scale_s, turned):
    root = HEAD_DIMENSION**-0.5
    lane_head = lax.broadcasted_iota(jnp.int32, (LANES, LANES), 1) % HEADS
    row_head = lax.broadcasted_iota(jnp.int32, (LANES, LANES), 0) % HEADS

    def fill(section, turned_offset, straight_offset):
        now = section % 2
        for head in range(HEADS):
            block, lane = head_place(head)
            own = pl.ds(head, MEM, stride=HEADS)
            for offset, target in ((turned_offset, key_rows), (straight_offset, value_rows)):
                start = offset + lane
                target[now, own, :] = kv_ref[slot(section), block, :, start : start + 128].astype(F32)
        columns = key_rows[now].T
        rows = value_rows[now]
        for head in range(HEADS):
            lanes = slice(head * 128, head * 128 + 128)
            left[now, lanes, :] = jnp.where(lane_head == head, columns, 0.0).astype(BF16)
            right[now, :, lanes] = jnp.where(row_head == head, rows, 0.0).astype(BF16)

    fill(0, 0, 256)
    state = h_ref[...]
    for s in range(SECTIONS):
        wide = state.astype(F32)
        hs[s] = wide
        raw = wide_dot(state, left[s % 2])
        scale = lax.rsqrt(jnp.mean(wide * wide, axis=-1, keepdims=True) + 1e-06)
        scores = raw * (scale * root)
        ratios = [jnp.exp(jnp.minimum(o - scores, 80.0)) for o in others(scores)]
        p = 1.0 / (1.0 + tree(ratios))
        sc_s[s] = scores
        p_s[s] = p
        scale_s[s] = jnp.broadcast_to(scale, (TOKENS, LANES))
        if s + 1 < SECTIONS:
            fill(s + 1, 0, 256)
            state = (wide + exact_dot(p, right[s % 2])).astype(BF16)

    fill(SECTIONS - 1, 256, 0)
    grad = g_ref[...]
    for s in reversed(range(SECTIONS)):
        wide = grad.astype(F32)
        gs[s] = wide
        p = p_s[s]
        dp = wide_dot(grad, left[s % 2])
        weighted = p * dp
        ds = p * (dp - tree([weighted] + others(weighted)))
        scale = scale_s[s][:, :1]
        ds_s[s] = ds * (scale_s[s] * root)
        if s > 0:
            fill(s - 1, 256, 0)
            along = jnp.sum(ds * sc_s[s], axis=-1, keepdims=True) * (1.0 / WIDTH)
            du = exact_dot(ds * root, right[s % 2])
            grad = (wide + scale * (du - hs[s] * (scale * along))).astype(BF16)

    row_section = lax.broadcasted_iota(jnp.int32, (LANES, LANES), 0) >> 3
    lane_section = lax.broadcasted_iota(jnp.int32, (LANES, LANES), 1) >> 3
    same = row_section == lane_section
    for coefficients, factors, offset in ((ds_s, hs, 0), (p_s, gs, 256)):
        turned[...] = coefficients[...].reshape(SECTIONS * TOKENS, LANES).T
        for head in range(HEADS):
            mine = turned[pl.ds(head, MEM, stride=HEADS), :]
            spread_out = jnp.broadcast_to(mine[None], (SECTIONS, MEM, LANES)).reshape(LANES, LANES)
            left = jnp.where(same, spread_out, 0.0).astype(BF16)
            lanes = slice(head * 128, head * 128 + 128)
            right = factors[:, :, lanes].reshape(SECTIONS * TOKENS, 128).astype(BF16)
            result = wide_dot(left, right).astype(BF16).reshape(SECTIONS, MEM, 128)
            block, lane = head_place(head)
            start = offset + lane
            for s in range(SECTIONS):
                out_ref[slot(s), block, :, start : start + 128] = result[s]


def chain(h, g, kv):
    vmem = pl.BlockSpec(memory_space=pltpu.VMEM)
    return pl.pallas_call(
        chain_kernel,
        out_shape=jax.ShapeDtypeStruct((SECTIONS, 8, MEM, 512), BF16),
        in_specs=[vmem] * 3,
        out_specs=vmem,
        scratch_shapes=[
            pltpu.VMEM((2, WIDTH, LANES), BF16),
            pltpu.VMEM((2, LANES, WIDTH), BF16),
            pltpu.VMEM((2, LANES, LANES), F32),
            pltpu.VMEM((2, LANES, LANES), F32),
            pltpu.VMEM((SECTIONS, TOKENS, WIDTH), F32),
            pltpu.VMEM((SECTIONS, TOKENS, WIDTH), F32),
            pltpu.VMEM((SECTIONS, TOKENS, LANES), F32),
            pltpu.VMEM((SECTIONS, TOKENS, LANES), F32),
            pltpu.VMEM((SECTIONS, TOKENS, LANES), F32),
            pltpu.VMEM((SECTIONS, TOKENS, LANES), F32),
            pltpu.VMEM((LANES, LANES), F32),
        ],
        compiler_params=pltpu.CompilerParams(vmem_limit_bytes=24 * 1024 * 1024),
        name="sections",
    )(h, g, kv)


def term_kernel(grad_ref, *refs):
    *weight_refs, out_ref, wide = refs
    rows = grad_ref.shape[1]
    for start in range(0, WIDTH, 512):
        columns = slice(start, start + 512)
        total = sum(rows_dot(grad_ref[i], ref[columns, :]) for i, ref in enumerate(weight_refs))
        for lane in range(0, 512, 128):
            wide[pl.ds((start + lane) // 128, rows, stride=HEADS), :] = total[:, lane : lane + 128]
    out_ref[...] = wide[...].astype(BF16).reshape(rows, HEADS, 128)


def term(grads, weights):
    vmem = pl.BlockSpec(memory_space=pltpu.VMEM)
    rows = grads.shape[1]
    return pl.pallas_call(
        term_kernel,
        out_shape=jax.ShapeDtypeStruct((rows, HEADS, 128), BF16),
        in_specs=[vmem] * (1 + len(weights)),
        out_specs=vmem,
        scratch_shapes=[pltpu.VMEM((rows * HEADS, 128), F32)],
        compiler_params=pltpu.CompilerParams(vmem_limit_bytes=24 * 1024 * 1024),
        name="term",
    )(grads, *weights)


def swap(block, axis):
    return lax.ppermute(block, axis, [(0, 1), (1, 0)])


def exchange(block, axes):
    return lax.all_to_all(block, axes, split_axis=0, concat_axis=0, tiled=True)


def in_order(blocks, yl, c):
    a, b, d, e = blocks
    a, b = jnp.where(c == 0, a, b), jnp.where(c == 0, b, a)
    d, e = jnp.where(c == 0, d, e), jnp.where(c == 0, e, d)
    low = yl == 0
    return [jnp.where(low, a, d), jnp.where(low, b, e), jnp.where(low, d, a), jnp.where(low, e, b)]


def body(memory, decoder_in, key_weight, value_weight, top_grad):
    zh, x = lax.axis_index("zh"), lax.axis_index("x")
    yl, c = lax.axis_index("yl"), lax.axis_index("c")

    own = jnp.concatenate([key_weight[0], value_weight[0]], axis=1)
    near = swap(own, "c")
    far = swap(own, "yl")

    piece = memory.reshape(2, 2, 2, 2, 128).transpose(0, 1, 3, 2, 4).reshape(1, 16, 128)
    piece = jnp.broadcast_to(piece, (16, 16, 128))
    wide = exchange(piece, SECTION).transpose(1, 0, 2).reshape(1, 16, 2048)
    wide, near, far = lax.optimization_barrier((wide, near, far))
    weights = [own, near, far, swap(far, "c")]
    rows = exchange(jnp.broadcast_to(wide, (8, 16, 2048)), BLOCK).reshape(128, 2048)
    parts = [jnp.dot(rows, w, preferred_element_type=F32).astype(BF16) for w in weights]
    parts = in_order(parts, yl, c)
    projected = jnp.concatenate([q[:, :64] for q in parts] + [q[:, 64:] for q in parts], axis=1)

    columns = projected.reshape(8, 2, MEM, 512).transpose(1, 0, 2, 3)
    outgoing = jnp.broadcast_to(columns[:, None], (2, 2, 8, MEM, 512)).reshape(32, MEM, 512)
    held = exchange(outgoing, ("zh",) + BLOCK).reshape(1, 4, 8, MEM, 512)
    kv = exchange(jnp.broadcast_to(held, (4, 4, 8, MEM, 512)), "x").reshape(16, 8, MEM, 512)

    mine = (zh // 2, (zh % 2 * 4 + x) * TOKENS, 0)
    h = lax.dynamic_slice(decoder_in, mine, (1, TOKENS, WIDTH))[0]
    g = lax.dynamic_slice(top_grad, mine, (1, TOKENS, WIDTH))[0]
    grads = chain(h, g, kv)

    shares = exchange(grads.reshape(4, 4, 8, MEM, 512), "x")
    summed = jnp.sum(shares.astype(F32), axis=0).astype(BF16)
    parts = exchange(summed.reshape(128, 2, 512), ("zh", "yh", "zl", "yl", "c"))
    parts = jnp.sum(parts.reshape(2, 2, 4, 2, 2, 2, 2, 512).astype(F32), axis=1).astype(BF16)
    back = parts.transpose(1, 3, 2, 4, 0, 5, 6).reshape(128, 2, 4, 64)
    members = [back[:, :, i].reshape(128, 128) for i in range(4)]
    members = jnp.stack(in_order(members, yl, c))
    pieces = exchange(term(members, weights), RING)
    return jnp.sum(pieces.astype(F32), axis=0).reshape(1, WIDTH)


def solution(mesh):
    fine = Mesh(mesh.devices.reshape(4, 4, 4, 2, 2, 2), SECTION + DP)
    placed = (
        P(DP, None, SECTION),
        P(DP, None, None),
        P(SECTION, None, DP),
        P(SECTION, None, DP),
        P(DP, None, None),
    )
    return jax.shard_map(
        body, mesh=fine, in_specs=placed, out_specs=P(SECTION + DP, None), check_vma=False
    )
```

time: 201 us -> 180 us (0.90)
  the two profiles are of different devices: /device:TPU:1 before, /device:TPU:8 now
where the time goes in v3:
time: 180 us; the launch traced here: 179 us
  blocking collectives  104 us (58%)
  waiting for transfers between devices  25.9 us (14%)
  starting transfers between devices  23.2 us (13%)
  Pallas kernels  15.8 us (9%)
  local copies, waits for them, and re-layouts  5.95 us (3%)
  other arithmetic  2.52 us (1%)
    all_to_all x5, blocking collectives, exchange(): return lax.all_to_all(block, axes, split_axis=0, concat_axis=0, tiled=True)  104 us
    all_to_all x2, waiting for transfers between devices, exchange(): return lax.all_to_all(block, axes, split_axis=0, concat_axis=0, tiled=True)  25.9 us
    pallas_call x1, Pallas kernels, chain(): pl.pallas_call(chain_kernel, out_shape=jax.ShapeDtypeStruct((SECTIONS, 8,...  15.1 us
    all_to_all x2, starting transfers between devices, exchange(): return lax.all_to_all(block, axes, split_axis=0, concat_axis=0, tiled=True)  11.7 us
    ppermute x3, starting transfers between devices, swap(): return lax.ppermute(block, axis, [(0, 1), (1, 0)])  11.6 us
  transfers between devices with their start and end apart: 5, of which 2 were waited for; matrix products, arithmetic and copies ran while one was open for 1% of the time, Pallas kernels for 0%

profile of v3, /device:TPU:8, one launch (start us, length us, event | category | flops | bytes accessed | tf_op | source)
XLA Modules:
  0.0 179.1 jit_solution(17733016449087262989)
XLA Ops:
  0.0 0.0 copy-start
  0.0 1.3 copy.53
  1.3 0.0 copy-done
  1.3 0.3 copy.54
  1.6 0.0 copy-start.1
  1.6 0.3 pad_maximum_fusion.refs_0_
  1.9 1.9 %collective-permute-start = (bf16[2048,128]{1,0:T(8,128)(2,1)S(1)}, bf16[2048,128]{1,0:T(8,128)(2,1)S(1)}, u32[]{:S(2)}, u32[]{:S(2)}) collective-permute-start(bf16[2048,128]{1,0:T(8,128)(2,1)S(1)} %pad_maximum_fusion.refs_0_), channel_id=1, source_target_pairs={{0,1},{1,0},{2,3},{3,2},{4,5},{5,4},{6,7},{7,6},{8,9},{9,8},{10,11... | collective-permute-start | bytes 1572872 | tf_op jit(solution)/shard_map/ppermute | solution.py:185
  3.8 7.7 %collective-permute-start.1 = (bf16[2048,128]{1,0:T(8,128)(2,1)S(1)}, bf16[2048,128]{1,0:T(8,128)(2,1)S(1)}, u32[]{:S(2)}, u32[]{:S(2)}) collective-permute-start(bf16[2048,128]{1,0:T(8,128)(2,1)S(1)} %pad_maximum_fusion.refs_0_), channel_id=1, source_target_pairs={{0,4},{4,0},{1,5},{5,1},{2,6},{6,2},{3,7},{7,3},{8,12},{12,8},{9,1... | collective-permute-start | bytes 1572872 | tf_op jit(solution)/shard_map/ppermute | solution.py:185
  11.5 0.0 copy-done.1
  11.6 17.5 %all_to_all.35 = bf16[16,16,128]{2,1,0:T(8,128)(2,1)S(1)} all-to-all(bf16[16,16,128]{2,1,0:T(8,128)(2,1)S(1)} %broadcast_in_dim.28), channel_id=1, replica_groups=mesh['zh'=4,'x'=4,'yh'=4,'yl'=2,'zl'=2,'c'=2] {'zh','x'}, dimensions={0} | all-to-all | bytes 131072 | tf_op jit(solution)/shard_map/all_to_all | solution.py:189
  29.1 0.0 collective-permute-done.refs_1_
  29.1 0.0 collective-permute-done.1.refs_2_
  29.1 0.8 broadcast_in_dim.30
  30.0 8.0 %all-to-all-start.1 = ((bf16[8,16,2048]{2,1,0:T(8,128)(2,1)}), bf16[8,16,2048]{2,1,0:T(8,128)(2,1)S(1)}, u32[]{:S(2)}, u32[]{:S(2)}) async-start(bf16[8,16,2048]{2,1,0:T(8,128)(2,1)} %broadcast_in_dim.30), calls=%async_computation.1 | async-start | bytes 1048576 | tf_op jit(solution)/shard_map/all_to_all | solution.py:189
  37.9 1.9 %collective-permute-start.2 = (bf16[2048,128]{1,0:T(8,128)(2,1)S(1)}, bf16[2048,128]{1,0:T(8,128)(2,1)S(1)}, u32[]{:S(2)}, u32[]{:S(2)}) collective-permute-start(bf16[2048,128]{1,0:T(8,128)(2,1)S(1)} %collective-permute-done.1.refs_2_), channel_id=1, source_target_pairs={{0,1},{1,0},{2,3},{3,2},{4,5},{5,4},{6,7},{7,6},{8,9},{9,8},{10,11... | collective-permute-start | bytes 1572872 | tf_op jit(solution)/shard_map/ppermute | solution.py:185
  39.9 13.6 %all-to-all-done.1 = bf16[8,16,2048]{2,1,0:T(8,128)(2,1)S(1)} async-done(((bf16[8,16,2048]{2,1,0:T(8,128)(2,1)}), bf16[8,16,2048]{2,1,0:T(8,128)(2,1)S(1)}, u32[]{:S(2)}, u32[]{:S(2)}) %all-to-all-start.1) | async-done | bytes 524320 | tf_op jit(solution)/shard_map/all_to_all | solution.py:189
  53.4 0.3 convolution_convert_fusion.1
  53.8 0.4 convolution_convert_fusion.3
  54.1 0.0 collective-permute-done.2.refs_3_
  54.1 0.4 convolution_convert_fusion
  54.5 0.4 broadcast_select_fusion.12
  55.0 0.1 copy.55
  55.1 17.9 %all_to_all.36 = bf16[32,8,512]{2,1,0:T(8,128)(2,1)S(1)} all-to-all(bf16[32,8,512]{2,1,0:T(8,128)(2,1)S(1)} %bitcast.49), channel_id=1, replica_groups=mesh['zh'=4,'x'=4,'yh'=4,'yl'=2,'zl'=2,'c'=2] {'zh','yh','zl'}, dimensions={0} | all-to-all | bytes 524288 | tf_op jit(solution)/shard_map/all_to_all | solution.py:189
  73.0 1.1 broadcast_in_dim.33
  74.1 3.7 %all-to-all-start.3 = ((bf16[4,4,8,8,512]{4,3,2,1,0:T(8,128)(2,1)}), bf16[4,4,8,8,512]{4,3,2,1,0:T(8,128)(2,1)S(1)}, u32[]{:S(2)}, u32[]{:S(2)}) async-start(bf16[4,4,8,8,512]{4,3,2,1,0:T(8,128)(2,1)} %broadcast_in_dim.33), calls=%async_computation.3 | async-start | bytes 2097152 | tf_op jit(solution)/shard_map/all_to_all | solution.py:189
  77.8 0.8 dynamic-slice_bitcast_fusion
  78.6 12.3 %all-to-all-done.3 = bf16[4,4,8,8,512]{4,3,2,1,0:T(8,128)(2,1)S(1)} async-done(((bf16[4,4,8,8,512]{4,3,2,1,0:T(8,128)(2,1)}), bf16[4,4,8,8,512]{4,3,2,1,0:T(8,128)(2,1)S(1)}, u32[]{:S(2)}, u32[]{:S(2)}) %all-to-all-start.3) | async-done | bytes 1048608 | tf_op jit(solution)/shard_map/all_to_all | solution.py:189
  90.9 15.1 %sections.1 = bf16[16,8,8,512]{3,2,1,0:T(8,128)(2,1)S(1)} custom-call(bf16[8,2048]{1,0:T(8,128)(2,1)S(1)} %get-tuple-element.20.h_ref, bf16[8,2048]{1,0:T(8,128)(2,1)S(1)} %get-tuple-element.19.g_ref, bf16[16,8,8,512]{3,2,1,0:T(8,128)(2,1)S(1)} %bitcast.39), custom_call_target="tpu_custom_call" | custom-call | tf_op jit(solution)/shard_map/sections/pallas_call | solution.py:136
  106.0 14.6 %all_to_all.37 = bf16[4,4,8,8,512]{4,3,2,1,0:T(8,128)(2,1)S(1)} all-to-all(bf16[4,4,8,8,512]{4,3,2,1,0:T(8,128)(2,1)S(1)} %bitcast.40), channel_id=1, replica_groups=mesh['zh'=4,'x'=4,'yh'=4,'yl'=2,'zl'=2,'c'=2] {'x'}, dimensions={0} | all-to-all | bytes 2097152 | tf_op jit(solution)/shard_map/all_to_all | solution.py:189
  120.6 0.2 reduce_sum.33
  120.8 0.1 reshape.173
  120.9 24.8 %all_to_all.38 = bf16[128,2,512]{2,1,0:T(2,128)(2,1)S(1)} all-to-all(bf16[128,2,512]{2,1,0:T(2,128)(2,1)S(1)} %reshape.173), channel_id=1, replica_groups=mesh['zh'=4,'x'=4,'yh'=4,'yl'=2,'zl'=2,'c'=2] {'zh','yh','zl','yl','c'}, dimensions={0} | all-to-all | bytes 524288 | tf_op jit(solution)/shard_map/all_to_all | solution.py:189
  145.7 0.5 reduce_sum.34
  146.2 0.1 copy.69
  146.4 0.1 copy.58
  146.5 0.2 reshape.175
  146.7 0.7 broadcast_select_fusion.7
  147.4 0.1 copy.59
  147.5 0.1 copy.63
  147.7 0.1 copy.60
  147.8 0.1 copy.64
  147.9 0.1 copy.61
  148.0 0.1 copy.65
  148.1 0.1 copy.62
  148.2 0.1 copy.66
  148.4 0.8 term.1
  149.2 29.2 %all_to_all.39 = bf16[128,16,128]{2,1,0:T(8,128)(2,1)S(1)} all-to-all(bf16[128,16,128]{2,1,0:T(8,128)(2,1)S(1)} %term.1), channel_id=1, replica_groups=mesh['zh'=4,'x'=4,'yh'=4,'yl'=2,'zl'=2,'c'=2] {'zh','x','yh','zl'}, dimensions={0} | all-to-all | bytes 1048576 | tf_op jit(solution)/shard_map/all_to_all | solution.py:189
  178.4 0.7 convert_reduce_fusion
  (15 shorter events, 0.2 us)
Async XLA Ops:
  0.0 1.3 copy-start
  1.6 10.0 %copy-start.1 = (bf16[2,8,128]{2,1,0:T(8,128)(2,1)S(1)}, bf16[2,8,128]{2,1,0:T(8,128)(2,1)}, u32[]{:S(2)}) copy-start(bf16[2,8,128]{2,1,0:T(8,128)(2,1)} %param.5) | copy-start | bytes 12292
  1.9 27.2 %collective-permute-start = (bf16[2048,128]{1,0:T(8,128)(2,1)S(1)}, bf16[2048,128]{1,0:T(8,128)(2,1)S(1)}, u32[]{:S(2)}, u32[]{:S(2)}) collective-permute-start(bf16[2048,128]{1,0:T(8,128)(2,1)S(1)} %pad_maximum_fusion.refs_0_), channel_id=1, source_target_pairs={{0,1},{1,0},{2,3},{3,2},{4,5},{5,4},{6,7},{7,6},{8,9},{9,8},{10,11... | collective-permute-start | bytes 1572872 | tf_op jit(solution)/shard_map/ppermute | solution.py:185
  3.8 25.3 %collective-permute-start.1 = (bf16[2048,128]{1,0:T(8,128)(2,1)S(1)}, bf16[2048,128]{1,0:T(8,128)(2,1)S(1)}, u32[]{:S(2)}, u32[]{:S(2)}) collective-permute-start(bf16[2048,128]{1,0:T(8,128)(2,1)S(1)} %pad_maximum_fusion.refs_0_), channel_id=1, source_target_pairs={{0,4},{4,0},{1,5},{5,1},{2,6},{6,2},{3,7},{7,3},{8,12},{12,8},{9,1... | collective-permute-start | bytes 1572872 | tf_op jit(solution)/shard_map/ppermute | solution.py:185
  30.0 23.5 %all-to-all-start.1 = ((bf16[8,16,2048]{2,1,0:T(8,128)(2,1)}), bf16[8,16,2048]{2,1,0:T(8,128)(2,1)S(1)}, u32[]{:S(2)}, u32[]{:S(2)}) async-start(bf16[8,16,2048]{2,1,0:T(8,128)(2,1)} %broadcast_in_dim.30), calls=%async_computation.1 | async-start | bytes 1048576 | tf_op jit(solution)/shard_map/all_to_all | solution.py:189
  37.9 16.2 %collective-permute-start.2 = (bf16[2048,128]{1,0:T(8,128)(2,1)S(1)}, bf16[2048,128]{1,0:T(8,128)(2,1)S(1)}, u32[]{:S(2)}, u32[]{:S(2)}) collective-permute-start(bf16[2048,128]{1,0:T(8,128)(2,1)S(1)} %collective-permute-done.1.refs_2_), channel_id=1, source_target_pairs={{0,1},{1,0},{2,3},{3,2},{4,5},{5,4},{6,7},{7,6},{8,9},{9,8},{10,11... | collective-permute-start | bytes 1572872 | tf_op jit(solution)/shard_map/ppermute | solution.py:185
  74.1 16.8 %all-to-all-start.3 = ((bf16[4,4,8,8,512]{4,3,2,1,0:T(8,128)(2,1)}), bf16[4,4,8,8,512]{4,3,2,1,0:T(8,128)(2,1)S(1)}, u32[]{:S(2)}, u32[]{:S(2)}) async-start(bf16[4,4,8,8,512]{4,3,2,1,0:T(8,128)(2,1)} %broadcast_in_dim.33), calls=%async_computation.3 | async-start | bytes 2097152 | tf_op jit(solution)/shard_map/all_to_all | solution.py:189

commit v4 on v3

--- a/solution.py
+++ b/solution.py
@@ -16,7 +16,6 @@
 SECTION = ("zh", "x")
 DP = ("yh", "yl", "zl", "c")
 BLOCK = ("yh", "zl")
-RING = SECTION + BLOCK
 F32 = jnp.float32
 BF16 = jnp.bfloat16
 
@@ -206,11 +205,12 @@
     far = swap(own, "yl")
 
     piece = memory.reshape(2, 2, 2, 2, 128).transpose(0, 1, 3, 2, 4).reshape(1, 16, 128)
-    piece = jnp.broadcast_to(piece, (16, 16, 128))
-    wide = exchange(piece, SECTION).transpose(1, 0, 2).reshape(1, 16, 2048)
-    wide, near, far = lax.optimization_barrier((wide, near, far))
+    narrow = exchange(jnp.broadcast_to(piece, (32, 16, 128)), ("zh",) + BLOCK)
+    narrow = narrow.reshape(4, 128, 128).transpose(1, 0, 2).reshape(1, 128, 512)
+    narrow, near, far = lax.optimization_barrier((narrow, near, far))
     weights = [own, near, far, swap(far, "c")]
-    rows = exchange(jnp.broadcast_to(wide, (8, 16, 2048)), BLOCK).reshape(128, 2048)
+    every = exchange(jnp.broadcast_to(narrow, (4, 128, 512)), "x")
+    rows = every.reshape(4, 128, 4, 128).transpose(1, 2, 0, 3).reshape(128, 2048)
     parts = [jnp.dot(rows, w, preferred_element_type=F32).astype(BF16) for w in weights]
     parts = in_order(parts, yl, c)
     projected = jnp.concatenate([q[:, :64] for q in parts] + [q[:, 64:] for q in parts], axis=1)
@@ -232,7 +232,9 @@
     back = parts.transpose(1, 3, 2, 4, 0, 5, 6).reshape(128, 2, 4, 64)
     members = [back[:, :, i].reshape(128, 128) for i in range(4)]
     members = jnp.stack(in_order(members, yl, c))
-    pieces = exchange(term(members, weights), RING)
+    pieces = term(members, weights).reshape(4, 4, 8, HEADS, 128).transpose(1, 0, 2, 3, 4)
+    pieces = jnp.sum(exchange(pieces, "x").astype(F32), axis=0).astype(BF16)
+    pieces = exchange(pieces.reshape(32, HEADS, 128), ("zh",) + BLOCK)
     return jnp.sum(pieces.astype(F32), axis=0).reshape(1, WIDTH)
 
 

time: 180 us -> 170 us (0.944)
  the two profiles are of different devices: /device:TPU:8 before, /device:TPU:1 now
where the time goes in v4:
time: 170 us; the launch traced here: 168 us
  blocking collectives  106 us (62%)
  starting transfers between devices  21.5 us (13%)
  Pallas kernels  15.8 us (9%)
  waiting for transfers between devices  14.5 us (9%)
  local copies, waits for them, and re-layouts  6.15 us (4%)
  other arithmetic  2.5 us (1%)
    all_to_all x6, blocking collectives, exchange(): return lax.all_to_all(block, axes, split_axis=0, concat_axis=0, tiled=True)  106 us
    pallas_call x1, Pallas kernels, chain(): pl.pallas_call(chain_kernel, out_shape=jax.ShapeDtypeStruct((SECTIONS, 8,...  15.1 us
    all_to_all x2, waiting for transfers between devices, exchange(): return lax.all_to_all(block, axes, split_axis=0, concat_axis=0, tiled=True)  14.5 us
    ppermute x3, starting transfers between devices, swap(): return lax.ppermute(block, axis, [(0, 1), (1, 0)])  13.8 us
    all_to_all x2, starting transfers between devices, exchange(): return lax.all_to_all(block, axes, split_axis=0, concat_axis=0, tiled=True)  7.71 us
  transfers between devices with their start and end apart: 5, of which 2 were waited for; matrix products, arithmetic and copies ran while one was open for 1% of the time, Pallas kernels for 0%

profile of v4, /device:TPU:1, one launch (start us, length us, event | category | flops | bytes accessed | tf_op | source)
XLA Modules:
  0.0 168.5 jit_solution(9979296510279727847)
XLA Ops:
  0.0 0.0 copy-start
  0.0 1.3 copy.73
  1.3 0.0 copy-done
  1.3 0.3 copy.74
  1.6 0.0 copy-start.1
  1.6 0.3 pad_maximum_fusion.refs_0_
  1.9 8.8 %collective-permute-start = (bf16[2048,128]{1,0:T(8,128)(2,1)S(1)}, bf16[2048,128]{1,0:T(8,128)(2,1)S(1)}, u32[]{:S(2)}, u32[]{:S(2)}) collective-permute-start(bf16[2048,128]{1,0:T(8,128)(2,1)S(1)} %pad_maximum_fusion.refs_0_), channel_id=1, source_target_pairs={{0,1},{1,0},{2,3},{3,2},{4,5},{5,4},{6,7},{7,6},{8,9},{9,8},{10,11... | collective-permute-start | bytes 1572872 | tf_op jit(solution)/shard_map/ppermute | solution.py:184
  10.7 1.9 %collective-permute-start.1 = (bf16[2048,128]{1,0:T(8,128)(2,1)S(1)}, bf16[2048,128]{1,0:T(8,128)(2,1)S(1)}, u32[]{:S(2)}, u32[]{:S(2)}) collective-permute-start(bf16[2048,128]{1,0:T(8,128)(2,1)S(1)} %pad_maximum_fusion.refs_0_), channel_id=1, source_target_pairs={{0,4},{4,0},{1,5},{5,1},{2,6},{6,2},{3,7},{7,3},{8,12},{12,8},{9,1... | collective-permute-start | bytes 1572872 | tf_op jit(solution)/shard_map/ppermute | solution.py:184
  12.6 0.0 copy-done.1
  12.6 23.3 %all_to_all.40 = bf16[32,16,128]{2,1,0:T(8,128)(2,1)S(1)} all-to-all(bf16[32,16,128]{2,1,0:T(8,128)(2,1)S(1)} %broadcast_in_dim.28), channel_id=1, replica_groups=mesh['zh'=4,'x'=4,'yh'=4,'yl'=2,'zl'=2,'c'=2] {'zh','yh','zl'}, dimensions={0} | all-to-all | bytes 262144 | tf_op jit(solution)/shard_map/all_to_all | solution.py:188
  35.9 0.1 copy.72
  36.1 0.0 collective-permute-done.refs_1_
  36.1 0.0 collective-permute-done.1.refs_2_
  36.1 0.9 broadcast_in_dim.30
  36.9 4.0 %all-to-all-start.1 = ((bf16[4,128,512]{1,2,0:T(8,128)(2,1)}), bf16[4,128,512]{1,2,0:T(8,128)(2,1)S(1)}, u32[]{:S(2)}, u32[]{:S(2)}) async-start(bf16[4,128,512]{1,2,0:T(8,128)(2,1)} %broadcast_in_dim.30), calls=%async_computation.1 | async-start | bytes 1048576 | tf_op jit(solution)/shard_map/all_to_all | solution.py:188
  40.9 3.1 %collective-permute-start.2 = (bf16[2048,128]{1,0:T(8,128)(2,1)S(1)}, bf16[2048,128]{1,0:T(8,128)(2,1)S(1)}, u32[]{:S(2)}, u32[]{:S(2)}) collective-permute-start(bf16[2048,128]{1,0:T(8,128)(2,1)S(1)} %collective-permute-done.1.refs_2_), channel_id=1, source_target_pairs={{0,1},{1,0},{2,3},{3,2},{4,5},{5,4},{6,7},{7,6},{8,9},{9,8},{10,11... | collective-permute-start | bytes 1572872 | tf_op jit(solution)/shard_map/ppermute | solution.py:184
  44.0 5.0 %all-to-all-done.1 = bf16[4,128,512]{1,2,0:T(8,128)(2,1)S(1)} async-done(((bf16[4,128,512]{1,2,0:T(8,128)(2,1)}), bf16[4,128,512]{1,2,0:T(8,128)(2,1)S(1)}, u32[]{:S(2)}, u32[]{:S(2)}) %all-to-all-start.1) | async-done | bytes 524320 | tf_op jit(solution)/shard_map/all_to_all | solution.py:188
  49.0 0.4 convolution_convert_fusion.1
  49.4 0.4 convolution_convert_fusion.3
  49.8 0.0 collective-permute-done.2.refs_3_
  49.8 0.4 convolution_convert_fusion
  50.1 0.4 broadcast_select_fusion.12
  50.6 0.1 copy.76
  50.8 17.0 %all_to_all.41 = bf16[32,8,512]{2,1,0:T(8,128)(2,1)S(1)} all-to-all(bf16[32,8,512]{2,1,0:T(8,128)(2,1)S(1)} %bitcast.62), channel_id=1, replica_groups=mesh['zh'=4,'x'=4,'yh'=4,'yl'=2,'zl'=2,'c'=2] {'zh','yh','zl'}, dimensions={0} | all-to-all | bytes 524288 | tf_op jit(solution)/shard_map/all_to_all | solution.py:188
  67.7 1.1 broadcast_in_dim.33
  68.8 3.7 %all-to-all-start.3 = ((bf16[4,4,8,8,512]{4,3,2,1,0:T(8,128)(2,1)}), bf16[4,4,8,8,512]{4,3,2,1,0:T(8,128)(2,1)S(1)}, u32[]{:S(2)}, u32[]{:S(2)}) async-start(bf16[4,4,8,8,512]{4,3,2,1,0:T(8,128)(2,1)} %broadcast_in_dim.33), calls=%async_computation.3 | async-start | bytes 2097152 | tf_op jit(solution)/shard_map/all_to_all | solution.py:188
  72.5 0.8 dynamic-slice_bitcast_fusion
  73.3 9.6 %all-to-all-done.3 = bf16[4,4,8,8,512]{4,3,2,1,0:T(8,128)(2,1)S(1)} async-done(((bf16[4,4,8,8,512]{4,3,2,1,0:T(8,128)(2,1)}), bf16[4,4,8,8,512]{4,3,2,1,0:T(8,128)(2,1)S(1)}, u32[]{:S(2)}, u32[]{:S(2)}) %all-to-all-start.3) | async-done | bytes 1048608 | tf_op jit(solution)/shard_map/all_to_all | solution.py:188
  82.9 15.1 %sections.1 = bf16[16,8,8,512]{3,2,1,0:T(8,128)(2,1)S(1)} custom-call(bf16[8,2048]{1,0:T(8,128)(2,1)S(1)} %get-tuple-element.20.h_ref, bf16[8,2048]{1,0:T(8,128)(2,1)S(1)} %get-tuple-element.19.g_ref, bf16[16,8,8,512]{3,2,1,0:T(8,128)(2,1)S(1)} %bitcast.50), custom_call_target="tpu_custom_call" | custom-call | tf_op jit(solution)/shard_map/sections/pallas_call | solution.py:135
  98.0 12.2 %all_to_all.42 = bf16[4,4,8,8,512]{4,3,2,1,0:T(8,128)(2,1)S(1)} all-to-all(bf16[4,4,8,8,512]{4,3,2,1,0:T(8,128)(2,1)S(1)} %bitcast.51), channel_id=1, replica_groups=mesh['zh'=4,'x'=4,'yh'=4,'yl'=2,'zl'=2,'c'=2] {'x'}, dimensions={0} | all-to-all | bytes 2097152 | tf_op jit(solution)/shard_map/all_to_all | solution.py:188
  110.1 0.2 reduce_sum.45
  110.4 0.1 reshape.187
  110.5 26.3 %all_to_all.43 = bf16[128,2,512]{2,1,0:T(2,128)(2,1)S(1)} all-to-all(bf16[128,2,512]{2,1,0:T(2,128)(2,1)S(1)} %reshape.187), channel_id=1, replica_groups=mesh['zh'=4,'x'=4,'yh'=4,'yl'=2,'zl'=2,'c'=2] {'zh','yh','zl','yl','c'}, dimensions={0} | all-to-all | bytes 524288 | tf_op jit(solution)/shard_map/all_to_all | solution.py:188
  136.8 0.5 reduce_sum.46
  137.3 0.1 copy.93
  137.4 0.1 copy.79
  137.5 0.2 reshape.189
  137.7 0.7 broadcast_select_fusion.7
  138.5 0.1 copy.80
  138.6 0.1 copy.84
  138.7 0.1 copy.81
  138.8 0.1 copy.85
  138.9 0.1 copy.82
  139.0 0.1 copy.86
  139.2 0.1 copy.83
  139.3 0.1 copy.87
  139.4 0.8 term.1
  140.3 10.7 %all_to_all.44 = bf16[4,4,8,16,128]{4,3,2,1,0:T(8,128)(2,1)S(1)} all-to-all(bf16[4,4,8,16,128]{4,3,2,1,0:T(8,128)(2,1)S(1)} %bitcast.60), channel_id=1, replica_groups=mesh['zh'=4,'x'=4,'yh'=4,'yl'=2,'zl'=2,'c'=2] {'x'}, dimensions={0} | all-to-all | bytes 1048576 | tf_op jit(solution)/shard_map/all_to_all | solution.py:188
  151.0 0.1 reduce_sum.47
  151.1 16.8 %all_to_all.45 = bf16[32,16,128]{2,1,0:T(8,128)(2,1)S(1)} all-to-all(bf16[32,16,128]{2,1,0:T(8,128)(2,1)S(1)} %bitcast.68), channel_id=1, replica_groups=mesh['zh'=4,'x'=4,'yh'=4,'yl'=2,'zl'=2,'c'=2] {'zh','yh','zl'}, dimensions={0} | all-to-all | bytes 262144 | tf_op jit(solution)/shard_map/all_to_all | solution.py:188
  167.8 0.6 convert_reduce_fusion
  (15 shorter events, 0.2 us)
Async XLA Ops:
  0.0 1.3 copy-start
  1.6 11.0 %copy-start.1 = (bf16[2,8,128]{2,1,0:T(8,128)(2,1)S(1)}, bf16[2,8,128]{2,1,0:T(8,128)(2,1)}, u32[]{:S(2)}) copy-start(bf16[2,8,128]{2,1,0:T(8,128)(2,1)} %param.5) | copy-start | bytes 12292
  1.9 34.2 %collective-permute-start = (bf16[2048,128]{1,0:T(8,128)(2,1)S(1)}, bf16[2048,128]{1,0:T(8,128)(2,1)S(1)}, u32[]{:S(2)}, u32[]{:S(2)}) collective-permute-start(bf16[2048,128]{1,0:T(8,128)(2,1)S(1)} %pad_maximum_fusion.refs_0_), channel_id=1, source_target_pairs={{0,1},{1,0},{2,3},{3,2},{4,5},{5,4},{6,7},{7,6},{8,9},{9,8},{10,11... | collective-permute-start | bytes 1572872 | tf_op jit(solution)/shard_map/ppermute | solution.py:184
  10.7 25.4 %collective-permute-start.1 = (bf16[2048,128]{1,0:T(8,128)(2,1)S(1)}, bf16[2048,128]{1,0:T(8,128)(2,1)S(1)}, u32[]{:S(2)}, u32[]{:S(2)}) collective-permute-start(bf16[2048,128]{1,0:T(8,128)(2,1)S(1)} %pad_maximum_fusion.refs_0_), channel_id=1, source_target_pairs={{0,4},{4,0},{1,5},{5,1},{2,6},{6,2},{3,7},{7,3},{8,12},{12,8},{9,1... | collective-permute-start | bytes 1572872 | tf_op jit(solution)/shard_map/ppermute | solution.py:184
  36.9 12.1 %all-to-all-start.1 = ((bf16[4,128,512]{1,2,0:T(8,128)(2,1)}), bf16[4,128,512]{1,2,0:T(8,128)(2,1)S(1)}, u32[]{:S(2)}, u32[]{:S(2)}) async-start(bf16[4,128,512]{1,2,0:T(8,128)(2,1)} %broadcast_in_dim.30), calls=%async_computation.1 | async-start | bytes 1048576 | tf_op jit(solution)/shard_map/all_to_all | solution.py:188
  40.9 8.8 %collective-permute-start.2 = (bf16[2048,128]{1,0:T(8,128)(2,1)S(1)}, bf16[2048,128]{1,0:T(8,128)(2,1)S(1)}, u32[]{:S(2)}, u32[]{:S(2)}) collective-permute-start(bf16[2048,128]{1,0:T(8,128)(2,1)S(1)} %collective-permute-done.1.refs_2_), channel_id=1, source_target_pairs={{0,1},{1,0},{2,3},{3,2},{4,5},{5,4},{6,7},{7,6},{8,9},{9,8},{10,11... | collective-permute-start | bytes 1572872 | tf_op jit(solution)/shard_map/ppermute | solution.py:184
  68.8 14.1 %all-to-all-start.3 = ((bf16[4,4,8,8,512]{4,3,2,1,0:T(8,128)(2,1)}), bf16[4,4,8,8,512]{4,3,2,1,0:T(8,128)(2,1)S(1)}, u32[]{:S(2)}, u32[]{:S(2)}) async-start(bf16[4,4,8,8,512]{4,3,2,1,0:T(8,128)(2,1)} %broadcast_in_dim.33), calls=%async_computation.3 | async-start | bytes 2097152 | tf_op jit(solution)/shard_map/all_to_all | solution.py:188

commit v5 on v4

--- a/solution.py
+++ b/solution.py
@@ -155,29 +155,42 @@
     )(h, g, kv)
 
 
-def term_kernel(grad_ref, *refs):
+def term_kernel(me_ref, part_ref, *refs):
     *weight_refs, out_ref, wide = refs
-    rows = grad_ref.shape[1]
+    yl_set, c_set = me_ref[0] == 1, me_ref[1] == 1
+    halves = part_ref[...].astype(F32).reshape(2, 2, 64, 512)
+    summed = (halves[:, 0] + halves[:, 1]).reshape(128, 512)
+    blocks = [
+        jnp.concatenate([summed[:, 64 * q : 64 * q + 64], summed[:, 256 + 64 * q : 320 + 64 * q]], axis=1)
+        for q in range(4)
+    ]
+    a, b, d, e = blocks
+    a, b = jnp.where(c_set, b, a), jnp.where(c_set, a, b)
+    d, e = jnp.where(c_set, e, d), jnp.where(c_set, d, e)
+    a, b, d, e = jnp.where(yl_set, d, a), jnp.where(yl_set, e, b), jnp.where(yl_set, a, d), jnp.where(yl_set, b, e)
+    grads = [q.astype(BF16) for q in (a, b, d, e)]
     for start in range(0, WIDTH, 512):
         columns = slice(start, start + 512)
-        total = sum(rows_dot(grad_ref[i], ref[columns, :]) for i, ref in enumerate(weight_refs))
+        total = sum(rows_dot(q, ref[columns, :]) for q, ref in zip(grads, weight_refs))
         for lane in range(0, 512, 128):
-            wide[pl.ds((start + lane) // 128, rows, stride=HEADS), :] = total[:, lane : lane + 128]
-    out_ref[...] = wide[...].astype(BF16).reshape(rows, HEADS, 128)
-
-
-def term(grads, weights):
+            wide[pl.ds((start + lane) // 128, 128, stride=HEADS), :] = total[:, lane : lane + 128]
+    for row in range(128):
+        j, yh, zl, yl, c, m = (row >> k & n for k, n in ((6, 1), (4, 3), (3, 1), (2, 1), (1, 1), (0, 1)))
+        owner = ((yl * 2 + zl) * 4 + yh) * 8 + (c * 2 + j) * 2 + m
+        out_ref[owner] = wide[row * HEADS : (row + 1) * HEADS, :].astype(BF16)
+
+
+def term(me, parts, weights):
     vmem = pl.BlockSpec(memory_space=pltpu.VMEM)
-    rows = grads.shape[1]
     return pl.pallas_call(
         term_kernel,
-        out_shape=jax.ShapeDtypeStruct((rows, HEADS, 128), BF16),
-        in_specs=[vmem] * (1 + len(weights)),
+        out_shape=jax.ShapeDtypeStruct((128, HEADS, 128), BF16),
+        in_specs=[pl.BlockSpec(memory_space=pltpu.SMEM)] + [vmem] * (1 + len(weights)),
         out_specs=vmem,
-        scratch_shapes=[pltpu.VMEM((rows * HEADS, 128), F32)],
+        scratch_shapes=[pltpu.VMEM((128 * HEADS, 128), F32)],
         compiler_params=pltpu.CompilerParams(vmem_limit_bytes=24 * 1024 * 1024),
         name="term",
-    )(grads, *weights)
+    )(me, parts, *weights)
 
 
 def swap(block, axis):
@@ -227,12 +240,8 @@
 
     shares = exchange(grads.reshape(4, 4, 8, MEM, 512), "x")
     summed = jnp.sum(shares.astype(F32), axis=0).astype(BF16)
-    parts = exchange(summed.reshape(128, 2, 512), ("zh", "yh", "zl", "yl", "c"))
-    parts = jnp.sum(parts.reshape(2, 2, 4, 2, 2, 2, 2, 512).astype(F32), axis=1).astype(BF16)
-    back = parts.transpose(1, 3, 2, 4, 0, 5, 6).reshape(128, 2, 4, 64)
-    members = [back[:, :, i].reshape(128, 128) for i in range(4)]
-    members = jnp.stack(in_order(members, yl, c))
-    pieces = term(members, weights).reshape(4, 4, 8, HEADS, 128).transpose(1, 0, 2, 3, 4)
+    parts = exchange(summed.reshape(128, 2, 512), ("zh", "yh", "zl", "yl", "c")).reshape(256, 512)
+    pieces = term(jnp.stack([yl, c]), parts, weights).reshape(4, 32, HEADS, 128)
     pieces = jnp.sum(exchange(pieces, "x").astype(F32), axis=0).astype(BF16)
     pieces = exchange(pieces.reshape(32, HEADS, 128), ("zh",) + BLOCK)
     return jnp.sum(pieces.astype(F32), axis=0).reshape(1, WIDTH)

time: 170 us -> 169 us (level)
  blocking collectives: 106 us -> 79.9 us
  waiting for transfers between devices: 14.5 us -> 28.6 us
  starting transfers between devices: 21.5 us -> 33.8 us
    all_to_all x6 -> x5, blocking collectives: 106 us -> 79.9 us  [exchange(): return lax.all_to_all(block, axes, split_axis=0, concat_axis=0, tiled=True)]
    all_to_all x2 -> x3, waiting for transfers between devices: 14.5 us -> 28.6 us  [exchange(): return lax.all_to_all(block, axes, split_axis=0, concat_axis=0, tiled=True)]
    all_to_all x2 -> x3, starting transfers between devices: 7.71 us -> 20.1 us  [exchange(): return lax.all_to_all(block, axes, split_axis=0, concat_axis=0, tiled=True)]
  transfers between devices with their start and end apart: 5 -> 6, of which waited for: 2 -> 3; matrix products, arithmetic and copies ran while one was open for 1% -> 1% of each run, Pallas kernels for 0% -> 0%
where the time goes in v5:
time: 169 us; the launch traced here: 167 us
  blocking collectives  79.9 us (47%)
  starting transfers between devices  33.8 us (20%)
  waiting for transfers between devices  28.6 us (17%)
  Pallas kernels  16.5 us (10%)
  local copies, waits for them, and re-layouts  5.57 us (3%)
    all_to_all x5, blocking collectives, exchange(): return lax.all_to_all(block, axes, split_axis=0, concat_axis=0, tiled=True)  79.9 us
    all_to_all x3, waiting for transfers between devices, exchange(): return lax.all_to_all(block, axes, split_axis=0, concat_axis=0, tiled=True)  28.6 us
    all_to_all x3, starting transfers between devices, exchange(): return lax.all_to_all(block, axes, split_axis=0, concat_axis=0, tiled=True)  20.1 us
    pallas_call x1, Pallas kernels, chain(): pl.pallas_call(chain_kernel, out_shape=jax.ShapeDtypeStruct((SECTIONS, 8,...  15.1 us
    ppermute x3, starting transfers between devices, swap(): return lax.ppermute(block, axis, [(0, 1), (1, 0)])  13.8 us
  transfers between devices with their start and end apart: 6, of which 3 were waited for; matrix products, arithmetic and copies ran while one was open for 1% of the time, Pallas kernels for 0%

profile of v5, /device:TPU:1, one launch (start us, length us, event | category | flops | bytes accessed | tf_op | source)
XLA Modules:
  0.0 167.4 jit_solution(8249439009429545713)
XLA Ops:
  0.0 0.0 copy-start
  0.0 1.3 copy.24
  1.3 0.0 copy-done
  1.3 0.3 copy.25
  1.6 0.0 copy-start.1
  1.6 0.3 pad_maximum_fusion.refs_0_
  1.9 8.8 %collective-permute-start = (bf16[2048,128]{1,0:T(8,128)(2,1)S(1)}, bf16[2048,128]{1,0:T(8,128)(2,1)S(1)}, u32[]{:S(2)}, u32[]{:S(2)}) collective-permute-start(bf16[2048,128]{1,0:T(8,128)(2,1)S(1)} %pad_maximum_fusion.refs_0_), channel_id=1, source_target_pairs={{0,1},{1,0},{2,3},{3,2},{4,5},{5,4},{6,7},{7,6},{8,9},{9,8},{10,11... | collective-permute-start | bytes 1572872 | tf_op jit(solution)/shard_map/ppermute | solution.py:197
  10.7 1.9 %collective-permute-start.1 = (bf16[2048,128]{1,0:T(8,128)(2,1)S(1)}, bf16[2048,128]{1,0:T(8,128)(2,1)S(1)}, u32[]{:S(2)}, u32[]{:S(2)}) collective-permute-start(bf16[2048,128]{1,0:T(8,128)(2,1)S(1)} %pad_maximum_fusion.refs_0_), channel_id=1, source_target_pairs={{0,4},{4,0},{1,5},{5,1},{2,6},{6,2},{3,7},{7,3},{8,12},{12,8},{9,1... | collective-permute-start | bytes 1572872 | tf_op jit(solution)/shard_map/ppermute | solution.py:197
  12.6 0.0 copy-done.1
  12.6 23.3 %all_to_all.40 = bf16[32,16,128]{2,1,0:T(8,128)(2,1)S(1)} all-to-all(bf16[32,16,128]{2,1,0:T(8,128)(2,1)S(1)} %broadcast_in_dim.28), channel_id=1, replica_groups=mesh['zh'=4,'x'=4,'yh'=4,'yl'=2,'zl'=2,'c'=2] {'zh','yh','zl'}, dimensions={0} | all-to-all | bytes 262144 | tf_op jit(solution)/shard_map/all_to_all | solution.py:201
  35.9 0.1 copy.23
  36.1 0.0 collective-permute-done.refs_1_
  36.1 0.0 collective-permute-done.1.refs_2_
  36.1 0.9 broadcast_in_dim.30
  36.9 4.0 %all-to-all-start.1 = ((bf16[4,128,512]{1,2,0:T(8,128)(2,1)}), bf16[4,128,512]{1,2,0:T(8,128)(2,1)S(1)}, u32[]{:S(2)}, u32[]{:S(2)}) async-start(bf16[4,128,512]{1,2,0:T(8,128)(2,1)} %broadcast_in_dim.30), calls=%async_computation.1 | async-start | bytes 1048576 | tf_op jit(solution)/shard_map/all_to_all | solution.py:201
  41.0 3.1 %collective-permute-start.2 = (bf16[2048,128]{1,0:T(8,128)(2,1)S(1)}, bf16[2048,128]{1,0:T(8,128)(2,1)S(1)}, u32[]{:S(2)}, u32[]{:S(2)}) collective-permute-start(bf16[2048,128]{1,0:T(8,128)(2,1)S(1)} %collective-permute-done.1.refs_2_), channel_id=1, source_target_pairs={{0,1},{1,0},{2,3},{3,2},{4,5},{5,4},{6,7},{7,6},{8,9},{9,8},{10,11... | collective-permute-start | bytes 1572872 | tf_op jit(solution)/shard_map/ppermute | solution.py:197
  44.0 5.0 %all-to-all-done.1 = bf16[4,128,512]{1,2,0:T(8,128)(2,1)S(1)} async-done(((bf16[4,128,512]{1,2,0:T(8,128)(2,1)}), bf16[4,128,512]{1,2,0:T(8,128)(2,1)S(1)}, u32[]{:S(2)}, u32[]{:S(2)}) %all-to-all-start.1) | async-done | bytes 524320 | tf_op jit(solution)/shard_map/all_to_all | solution.py:201
  49.1 0.4 convolution_convert_fusion.1
  49.4 0.4 convolution_convert_fusion.3
  49.8 0.0 collective-permute-done.2.refs_3_
  49.8 0.4 convolution_convert_fusion
  50.1 0.4 broadcast_select_fusion.4
  50.6 0.1 copy.27
  50.8 17.0 %all_to_all.41 = bf16[32,8,512]{2,1,0:T(8,128)(2,1)S(1)} all-to-all(bf16[32,8,512]{2,1,0:T(8,128)(2,1)S(1)} %bitcast.51), channel_id=1, replica_groups=mesh['zh'=4,'x'=4,'yh'=4,'yl'=2,'zl'=2,'c'=2] {'zh','yh','zl'}, dimensions={0} | all-to-all | bytes 524288 | tf_op jit(solution)/shard_map/all_to_all | solution.py:201
  67.7 1.1 broadcast_in_dim.33
  68.8 3.7 %all-to-all-start.3 = ((bf16[4,4,8,8,512]{4,3,2,1,0:T(8,128)(2,1)}), bf16[4,4,8,8,512]{4,3,2,1,0:T(8,128)(2,1)S(1)}, u32[]{:S(2)}, u32[]{:S(2)}) async-start(bf16[4,4,8,8,512]{4,3,2,1,0:T(8,128)(2,1)} %broadcast_in_dim.33), calls=%async_computation.3 | async-start | bytes 2097152 | tf_op jit(solution)/shard_map/all_to_all | solution.py:201
  72.5 0.8 dynamic-slice_bitcast_fusion
  73.3 9.6 %all-to-all-done.3 = bf16[4,4,8,8,512]{4,3,2,1,0:T(8,128)(2,1)S(1)} async-done(((bf16[4,4,8,8,512]{4,3,2,1,0:T(8,128)(2,1)}), bf16[4,4,8,8,512]{4,3,2,1,0:T(8,128)(2,1)S(1)}, u32[]{:S(2)}, u32[]{:S(2)}) %all-to-all-start.3) | async-done | bytes 1048608 | tf_op jit(solution)/shard_map/all_to_all | solution.py:201
  82.9 15.1 %sections.1 = bf16[16,8,8,512]{3,2,1,0:T(8,128)(2,1)S(1)} custom-call(bf16[8,2048]{1,0:T(8,128)(2,1)S(1)} %get-tuple-element.16.h_ref, bf16[8,2048]{1,0:T(8,128)(2,1)S(1)} %get-tuple-element.15.g_ref, bf16[16,8,8,512]{3,2,1,0:T(8,128)(2,1)S(1)} %bitcast.40), custom_call_target="tpu_custom_call" | custom-call | tf_op jit(solution)/shard_map/sections/pallas_call | solution.py:135
  98.0 12.2 %all_to_all.42 = bf16[4,4,8,8,512]{4,3,2,1,0:T(8,128)(2,1)S(1)} all-to-all(bf16[4,4,8,8,512]{4,3,2,1,0:T(8,128)(2,1)S(1)} %bitcast.41), channel_id=1, replica_groups=mesh['zh'=4,'x'=4,'yh'=4,'yl'=2,'zl'=2,'c'=2] {'x'}, dimensions={0} | all-to-all | bytes 2097152 | tf_op jit(solution)/shard_map/all_to_all | solution.py:201
  110.1 0.2 reduce_sum.33
  110.3 0.8 reshape.53
  111.1 12.4 %all-to-all-start.5 = ((bf16[128,2,512]{2,1,0:T(2,128)(2,1)}), bf16[128,2,512]{2,1,0:T(2,128)(2,1)S(1)}, u32[]{:S(2)}, u32[]{:S(2)}) async-start(bf16[128,2,512]{2,1,0:T(2,128)(2,1)} %reshape.53), calls=%async_computation.5 | async-start | bytes 524288 | tf_op jit(solution)/shard_map/all_to_all | solution.py:201
  123.5 0.1 pad_add_fusion.me_ref
  123.6 14.0 %all-to-all-done.5 = bf16[128,2,512]{2,1,0:T(2,128)(2,1)S(1)} async-done(((bf16[128,2,512]{2,1,0:T(2,128)(2,1)}), bf16[128,2,512]{2,1,0:T(2,128)(2,1)S(1)}, u32[]{:S(2)}, u32[]{:S(2)}) %all-to-all-start.5) | async-done | bytes 262176 | tf_op jit(solution)/shard_map/all_to_all | solution.py:201
  137.6 0.1 reshape.54.part_ref
  137.7 1.4 term.1
  139.2 10.7 %all_to_all.43 = bf16[4,32,16,128]{3,2,1,0:T(8,128)(2,1)S(1)} all-to-all(bf16[4,32,16,128]{3,2,1,0:T(8,128)(2,1)S(1)} %bitcast.42), channel_id=1, replica_groups=mesh['zh'=4,'x'=4,'yh'=4,'yl'=2,'zl'=2,'c'=2] {'x'}, dimensions={0} | all-to-all | bytes 1048576 | tf_op jit(solution)/shard_map/all_to_all | solution.py:201
  149.9 0.1 reduce_sum.34
  149.9 16.8 %all_to_all.44 = bf16[32,16,128]{2,1,0:T(8,128)(2,1)S(1)} all-to-all(bf16[32,16,128]{2,1,0:T(8,128)(2,1)S(1)} %reduce_sum.34), channel_id=1, replica_groups=mesh['zh'=4,'x'=4,'yh'=4,'yl'=2,'zl'=2,'c'=2] {'zh','yh','zl'}, dimensions={0} | all-to-all | bytes 262144 | tf_op jit(solution)/shard_map/all_to_all | solution.py:201
  166.7 0.6 convert_reduce_fusion
  (13 shorter events, 0.2 us)
Async XLA Ops:
  0.0 1.3 copy-start
  1.6 11.0 %copy-start.1 = (bf16[2,8,128]{2,1,0:T(8,128)(2,1)S(1)}, bf16[2,8,128]{2,1,0:T(8,128)(2,1)}, u32[]{:S(2)}) copy-start(bf16[2,8,128]{2,1,0:T(8,128)(2,1)} %param.5) | copy-start | bytes 12292
  1.9 34.2 %collective-permute-start = (bf16[2048,128]{1,0:T(8,128)(2,1)S(1)}, bf16[2048,128]{1,0:T(8,128)(2,1)S(1)}, u32[]{:S(2)}, u32[]{:S(2)}) collective-permute-start(bf16[2048,128]{1,0:T(8,128)(2,1)S(1)} %pad_maximum_fusion.refs_0_), channel_id=1, source_target_pairs={{0,1},{1,0},{2,3},{3,2},{4,5},{5,4},{6,7},{7,6},{8,9},{9,8},{10,11... | collective-permute-start | bytes 1572872 | tf_op jit(solution)/shard_map/ppermute | solution.py:197
  10.7 25.4 %collective-permute-start.1 = (bf16[2048,128]{1,0:T(8,128)(2,1)S(1)}, bf16[2048,128]{1,0:T(8,128)(2,1)S(1)}, u32[]{:S(2)}, u32[]{:S(2)}) collective-permute-start(bf16[2048,128]{1,0:T(8,128)(2,1)S(1)} %pad_maximum_fusion.refs_0_), channel_id=1, source_target_pairs={{0,4},{4,0},{1,5},{5,1},{2,6},{6,2},{3,7},{7,3},{8,12},{12,8},{9,1... | collective-permute-start | bytes 1572872 | tf_op jit(solution)/shard_map/ppermute | solution.py:197
  36.9 12.1 %all-to-all-start.1 = ((bf16[4,128,512]{1,2,0:T(8,128)(2,1)}), bf16[4,128,512]{1,2,0:T(8,128)(2,1)S(1)}, u32[]{:S(2)}, u32[]{:S(2)}) async-start(bf16[4,128,512]{1,2,0:T(8,128)(2,1)} %broadcast_in_dim.30), calls=%async_computation.1 | async-start | bytes 1048576 | tf_op jit(solution)/shard_map/all_to_all | solution.py:201
  41.0 8.8 %collective-permute-start.2 = (bf16[2048,128]{1,0:T(8,128)(2,1)S(1)}, bf16[2048,128]{1,0:T(8,128)(2,1)S(1)}, u32[]{:S(2)}, u32[]{:S(2)}) collective-permute-start(bf16[2048,128]{1,0:T(8,128)(2,1)S(1)} %collective-permute-done.1.refs_2_), channel_id=1, source_target_pairs={{0,1},{1,0},{2,3},{3,2},{4,5},{5,4},{6,7},{7,6},{8,9},{9,8},{10,11... | collective-permute-start | bytes 1572872 | tf_op jit(solution)/shard_map/ppermute | solution.py:197
  68.8 14.1 %all-to-all-start.3 = ((bf16[4,4,8,8,512]{4,3,2,1,0:T(8,128)(2,1)}), bf16[4,4,8,8,512]{4,3,2,1,0:T(8,128)(2,1)S(1)}, u32[]{:S(2)}, u32[]{:S(2)}) async-start(bf16[4,4,8,8,512]{4,3,2,1,0:T(8,128)(2,1)} %broadcast_in_dim.33), calls=%async_computation.3 | async-start | bytes 2097152 | tf_op jit(solution)/shard_map/all_to_all | solution.py:201
  111.1 26.5 %all-to-all-start.5 = ((bf16[128,2,512]{2,1,0:T(2,128)(2,1)}), bf16[128,2,512]{2,1,0:T(2,128)(2,1)S(1)}, u32[]{:S(2)}, u32[]{:S(2)}) async-start(bf16[128,2,512]{2,1,0:T(2,128)(2,1)} %reshape.53), calls=%async_computation.5 | async-start | bytes 524288 | tf_op jit(solution)/shard_map/all_to_all | solution.py:201

commit v6 on v5

--- a/solution.py
+++ b/solution.py
@@ -60,8 +60,8 @@
 
 def chain_kernel(h_ref, g_ref, kv_ref, out_ref, left, right, key_rows, value_rows, hs, gs, sc_s, p_s, ds_s, scale_s, turned):
     root = HEAD_DIMENSION**-0.5
-    lane_head = lax.broadcasted_iota(jnp.int32, (LANES, LANES), 1) % HEADS
-    row_head = lax.broadcasted_iota(jnp.int32, (LANES, LANES), 0) % HEADS
+    lane_head = lax.broadcasted_iota(jnp.int32, (HEADS, LANES), 1) % HEADS
+    row_head = lax.broadcasted_iota(jnp.int32, (HEADS, LANES), 0)
 
     def fill(section, turned_offset, straight_offset):
         now = section % 2
@@ -71,12 +71,14 @@
             for offset, target in ((turned_offset, key_rows), (straight_offset, value_rows)):
                 start = offset + lane
                 target[now, own, :] = kv_ref[slot(section), block, :, start : start + 128].astype(F32)
-        columns = key_rows[now].T
-        rows = value_rows[now]
+        columns = key_rows[now].T.astype(BF16).reshape(MEM, HEADS, LANES)
+        rows = value_rows[now].astype(BF16).reshape(MEM, HEADS, LANES)
         for head in range(HEADS):
             lanes = slice(head * 128, head * 128 + 128)
-            left[now, lanes, :] = jnp.where(lane_head == head, columns, 0.0).astype(BF16)
-            right[now, :, lanes] = jnp.where(row_head == head, rows, 0.0).astype(BF16)
+            lane_mask = (lane_head == head).astype(F32).astype(BF16)
+            row_mask = (row_head == head).astype(F32).astype(BF16)
+            left[now, lanes, :] = (columns * lane_mask[None]).reshape(LANES, LANES)
+            right[now, :, lanes] = (rows * row_mask[None]).reshape(LANES, LANES)
 
     fill(0, 0, 256)
     state = h_ref[...]
@@ -217,12 +219,17 @@
     near = swap(own, "c")
     far = swap(own, "yl")
 
+    mine = (zh // 2, (zh % 2 * 4 + x) * TOKENS, 0)
+    h = lax.dynamic_slice(decoder_in, mine, (1, TOKENS, WIDTH))[0]
+    g = lax.dynamic_slice(top_grad, mine, (1, TOKENS, WIDTH))[0]
+
     piece = memory.reshape(2, 2, 2, 2, 128).transpose(0, 1, 3, 2, 4).reshape(1, 16, 128)
     narrow = exchange(jnp.broadcast_to(piece, (32, 16, 128)), ("zh",) + BLOCK)
     narrow = narrow.reshape(4, 128, 128).transpose(1, 0, 2).reshape(1, 128, 512)
     narrow, near, far = lax.optimization_barrier((narrow, near, far))
     weights = [own, near, far, swap(far, "c")]
     every = exchange(jnp.broadcast_to(narrow, (4, 128, 512)), "x")
+    every, h, g, me = lax.optimization_barrier((every, h, g, jnp.stack([yl, c])))
     rows = every.reshape(4, 128, 4, 128).transpose(1, 2, 0, 3).reshape(128, 2048)
     parts = [jnp.dot(rows, w, preferred_element_type=F32).astype(BF16) for w in weights]
     parts = in_order(parts, yl, c)
@@ -233,15 +240,12 @@
     held = exchange(outgoing, ("zh",) + BLOCK).reshape(1, 4, 8, MEM, 512)
     kv = exchange(jnp.broadcast_to(held, (4, 4, 8, MEM, 512)), "x").reshape(16, 8, MEM, 512)
 
-    mine = (zh // 2, (zh % 2 * 4 + x) * TOKENS, 0)
-    h = lax.dynamic_slice(decoder_in, mine, (1, TOKENS, WIDTH))[0]
-    g = lax.dynamic_slice(top_grad, mine, (1, TOKENS, WIDTH))[0]
     grads = chain(h, g, kv)
 
     shares = exchange(grads.reshape(4, 4, 8, MEM, 512), "x")
     summed = jnp.sum(shares.astype(F32), axis=0).astype(BF16)
     parts = exchange(summed.reshape(128, 2, 512), ("zh", "yh", "zl", "yl", "c")).reshape(256, 512)
-    pieces = term(jnp.stack([yl, c]), parts, weights).reshape(4, 32, HEADS, 128)
+    pieces = term(me, parts, weights).reshape(4, 32, HEADS, 128)
     pieces = jnp.sum(exchange(pieces, "x").astype(F32), axis=0).astype(BF16)
     pieces = exchange(pieces.reshape(32, HEADS, 128), ("zh",) + BLOCK)
     return jnp.sum(pieces.astype(F32), axis=0).reshape(1, WIDTH)

time: 169 us -> 168 us (level)
  blocking collectives: 79.9 us -> 122 us
  waiting for transfers between devices: 28.6 us -> 2.74 us
  starting transfers between devices: 33.8 us -> 18.5 us
    all_to_all x5 -> x7, blocking collectives: 79.9 us -> 122 us  [exchange(): return lax.all_to_all(block, axes, split_axis=0, concat_axis=0, tiled=True)]
    all_to_all x3 -> x1, waiting for transfers between devices: 28.6 us -> 2.74 us  [exchange(): return lax.all_to_all(block, axes, split_axis=0, concat_axis=0, tiled=True)]
    all_to_all x3 -> x1, starting transfers between devices: 20.1 us -> 4.01 us  [exchange(): return lax.all_to_all(block, axes, split_axis=0, concat_axis=0, tiled=True)]
  transfers between devices with their start and end apart: 6 -> 4, of which waited for: 3 -> 1; matrix products, arithmetic and copies ran while one was open for 1% -> 1% of each run, Pallas kernels for 0% -> 0%
where the time goes in v6:
time: 168 us; the launch traced here: 166 us
  blocking collectives  122 us (73%)
  starting transfers between devices  18.5 us (11%)
  Pallas kernels  15.6 us (9%)
  local copies, waits for them, and re-layouts  3.89 us (2%)
  waiting for transfers between devices  2.74 us (2%)
    all_to_all x7, blocking collectives, exchange(): return lax.all_to_all(block, axes, split_axis=0, concat_axis=0, tiled=True)  122 us
    ppermute x3, starting transfers between devices, swap(): return lax.ppermute(block, axis, [(0, 1), (1, 0)])  14.5 us
    pallas_call x1, Pallas kernels, chain(): pl.pallas_call(chain_kernel, out_shape=jax.ShapeDtypeStruct((SECTIONS, 8,...  14.2 us
    all_to_all x1, starting transfers between devices, exchange(): return lax.all_to_all(block, axes, split_axis=0, concat_axis=0, tiled=True)  4.01 us
  transfers between devices with their start and end apart: 4, of which 1 were waited for; matrix products, arithmetic and copies ran while one was open for 1% of the time, Pallas kernels for 0%

profile of v6, /device:TPU:1, one launch (start us, length us, event | category | flops | bytes accessed | tf_op | source)
XLA Modules:
  0.0 165.8 jit_solution(4855146665558393377)
XLA Ops:
  0.0 0.0 copy-start
  0.0 1.3 copy.24
  1.3 0.0 copy-done
  1.3 0.3 copy.25
  1.6 0.0 copy-start.1
  1.6 0.3 pad_maximum_fusion.refs_0_
  1.9 4.0 %collective-permute-start.1 = (bf16[2048,128]{1,0:T(8,128)(2,1)S(1)}, bf16[2048,128]{1,0:T(8,128)(2,1)S(1)}, u32[]{:S(2)}, u32[]{:S(2)}) collective-permute-start(bf16[2048,128]{1,0:T(8,128)(2,1)S(1)} %pad_maximum_fusion.refs_0_), channel_id=1, source_target_pairs={{0,4},{4,0},{1,5},{5,1},{2,6},{6,2},{3,7},{7,3},{8,12},{12,8},{9,1... | collective-permute-start | bytes 1572872 | tf_op jit(solution)/shard_map/ppermute | solution.py:199
  5.9 6.7 %collective-permute-start = (bf16[2048,128]{1,0:T(8,128)(2,1)S(1)}, bf16[2048,128]{1,0:T(8,128)(2,1)S(1)}, u32[]{:S(2)}, u32[]{:S(2)}) collective-permute-start(bf16[2048,128]{1,0:T(8,128)(2,1)S(1)} %pad_maximum_fusion.refs_0_), channel_id=1, source_target_pairs={{0,1},{1,0},{2,3},{3,2},{4,5},{5,4},{6,7},{7,6},{8,9},{9,8},{10,11... | collective-permute-start | bytes 1572872 | tf_op jit(solution)/shard_map/ppermute | solution.py:199
  12.6 0.0 copy-done.1
  12.6 22.3 %all_to_all.40 = bf16[32,16,128]{2,1,0:T(8,128)(2,1)S(1)} all-to-all(bf16[32,16,128]{2,1,0:T(8,128)(2,1)S(1)} %broadcast_in_dim.28), channel_id=1, replica_groups=mesh['zh'=4,'x'=4,'yh'=4,'yl'=2,'zl'=2,'c'=2] {'zh','yh','zl'}, dimensions={0} | all-to-all | bytes 262144 | tf_op jit(solution)/shard_map/all_to_all | solution.py:203
  34.9 0.1 copy.23
  35.0 0.0 collective-permute-done.1.refs_2_
  35.1 0.0 collective-permute-done.refs_1_
  35.1 0.9 broadcast_in_dim.30
  35.9 4.0 %all-to-all-start.1 = ((bf16[4,128,512]{1,2,0:T(8,128)(2,1)}), bf16[4,128,512]{1,2,0:T(8,128)(2,1)S(1)}, u32[]{:S(2)}, u32[]{:S(2)}) async-start(bf16[4,128,512]{1,2,0:T(8,128)(2,1)} %broadcast_in_dim.30), calls=%async_computation.1 | async-start | bytes 1048576 | tf_op jit(solution)/shard_map/all_to_all | solution.py:203
  39.9 0.8 dynamic-slice_bitcast_fusion
  40.7 3.8 %collective-permute-start.2 = (bf16[2048,128]{1,0:T(8,128)(2,1)S(1)}, bf16[2048,128]{1,0:T(8,128)(2,1)S(1)}, u32[]{:S(2)}, u32[]{:S(2)}) collective-permute-start(bf16[2048,128]{1,0:T(8,128)(2,1)S(1)} %collective-permute-done.1.refs_2_), channel_id=1, source_target_pairs={{0,1},{1,0},{2,3},{3,2},{4,5},{5,4},{6,7},{7,6},{8,9},{9,8},{10,11... | collective-permute-start | bytes 1572872 | tf_op jit(solution)/shard_map/ppermute | solution.py:199
  44.5 0.1 pad_add_fusion.me_ref
  44.6 2.7 %all-to-all-done.1 = bf16[4,128,512]{1,2,0:T(8,128)(2,1)S(1)} async-done(((bf16[4,128,512]{1,2,0:T(8,128)(2,1)}), bf16[4,128,512]{1,2,0:T(8,128)(2,1)S(1)}, u32[]{:S(2)}, u32[]{:S(2)}) %all-to-all-start.1) | async-done | bytes 524320 | tf_op jit(solution)/shard_map/all_to_all | solution.py:203
  47.3 0.4 convolution_convert_fusion.1
  47.7 0.4 convolution_convert_fusion.3
  48.1 0.0 collective-permute-done.2.refs_3_
  48.1 0.4 convolution_convert_fusion
  48.4 0.4 broadcast_select_fusion.4
  48.9 0.1 copy.27
  49.1 17.0 %all_to_all.41 = bf16[32,8,512]{2,1,0:T(8,128)(2,1)S(1)} all-to-all(bf16[32,8,512]{2,1,0:T(8,128)(2,1)S(1)} %bitcast.51), channel_id=1, replica_groups=mesh['zh'=4,'x'=4,'yh'=4,'yl'=2,'zl'=2,'c'=2] {'zh','yh','zl'}, dimensions={0} | all-to-all | bytes 524288 | tf_op jit(solution)/shard_map/all_to_all | solution.py:203
  66.1 0.1 broadcast_in_dim.33
  66.2 13.8 %all_to_all.42 = bf16[4,4,8,8,512]{4,3,2,1,0:T(8,128)(2,1)S(1)} all-to-all(bf16[4,4,8,8,512]{4,3,2,1,0:T(8,128)(2,1)S(1)} %broadcast_in_dim.33), channel_id=1, replica_groups=mesh['zh'=4,'x'=4,'yh'=4,'yl'=2,'zl'=2,'c'=2] {'x'}, dimensions={0} | all-to-all | bytes 2097152 | tf_op jit(solution)/shard_map/all_to_all | solution.py:203
  80.0 14.2 %sections.1 = bf16[16,8,8,512]{3,2,1,0:T(8,128)(2,1)S(1)} custom-call(bf16[8,2048]{1,0:T(8,128)(2,1)S(1)} %get-tuple-element.14.h_ref, bf16[8,2048]{1,0:T(8,128)(2,1)S(1)} %get-tuple-element.15.g_ref, bf16[16,8,8,512]{3,2,1,0:T(8,128)(2,1)S(1)} %bitcast.40), custom_call_target="tpu_custom_call" | custom-call | tf_op jit(solution)/shard_map/sections/pallas_call | solution.py:137
  94.2 12.9 %all_to_all.43 = bf16[4,4,8,8,512]{4,3,2,1,0:T(8,128)(2,1)S(1)} all-to-all(bf16[4,4,8,8,512]{4,3,2,1,0:T(8,128)(2,1)S(1)} %bitcast.41), channel_id=1, replica_groups=mesh['zh'=4,'x'=4,'yh'=4,'yl'=2,'zl'=2,'c'=2] {'x'}, dimensions={0} | all-to-all | bytes 2097152 | tf_op jit(solution)/shard_map/all_to_all | solution.py:203
  107.1 0.2 reduce_sum.33
  107.3 0.1 reshape.53
  107.4 28.7 %all_to_all.44 = bf16[128,2,512]{2,1,0:T(2,128)(2,1)S(1)} all-to-all(bf16[128,2,512]{2,1,0:T(2,128)(2,1)S(1)} %reshape.53), channel_id=1, replica_groups=mesh['zh'=4,'x'=4,'yh'=4,'yl'=2,'zl'=2,'c'=2] {'zh','yh','zl','yl','c'}, dimensions={0} | all-to-all | bytes 524288 | tf_op jit(solution)/shard_map/all_to_all | solution.py:203
  136.1 0.1 reshape.54.part_ref
  136.2 1.4 term.1
  137.6 10.7 %all_to_all.45 = bf16[4,32,16,128]{3,2,1,0:T(8,128)(2,1)S(1)} all-to-all(bf16[4,32,16,128]{3,2,1,0:T(8,128)(2,1)S(1)} %bitcast.42), channel_id=1, replica_groups=mesh['zh'=4,'x'=4,'yh'=4,'yl'=2,'zl'=2,'c'=2] {'x'}, dimensions={0} | all-to-all | bytes 1048576 | tf_op jit(solution)/shard_map/all_to_all | solution.py:203
  148.3 0.1 reduce_sum.34
  148.4 16.8 %all_to_all.46 = bf16[32,16,128]{2,1,0:T(8,128)(2,1)S(1)} all-to-all(bf16[32,16,128]{2,1,0:T(8,128)(2,1)S(1)} %reduce_sum.34), channel_id=1, replica_groups=mesh['zh'=4,'x'=4,'yh'=4,'yl'=2,'zl'=2,'c'=2] {'zh','yh','zl'}, dimensions={0} | all-to-all | bytes 262144 | tf_op jit(solution)/shard_map/all_to_all | solution.py:203
  165.2 0.6 convert_reduce_fusion
  (13 shorter events, 0.2 us)
Async XLA Ops:
  0.0 1.3 copy-start
  1.6 11.0 %copy-start.1 = (bf16[2,8,128]{2,1,0:T(8,128)(2,1)S(1)}, bf16[2,8,128]{2,1,0:T(8,128)(2,1)}, u32[]{:S(2)}) copy-start(bf16[2,8,128]{2,1,0:T(8,128)(2,1)} %param.5) | copy-start | bytes 12292
  1.9 33.2 %collective-permute-start.1 = (bf16[2048,128]{1,0:T(8,128)(2,1)S(1)}, bf16[2048,128]{1,0:T(8,128)(2,1)S(1)}, u32[]{:S(2)}, u32[]{:S(2)}) collective-permute-start(bf16[2048,128]{1,0:T(8,128)(2,1)S(1)} %pad_maximum_fusion.refs_0_), channel_id=1, source_target_pairs={{0,4},{4,0},{1,5},{5,1},{2,6},{6,2},{3,7},{7,3},{8,12},{12,8},{9,1... | collective-permute-start | bytes 1572872 | tf_op jit(solution)/shard_map/ppermute | solution.py:199
  5.9 29.1 %collective-permute-start = (bf16[2048,128]{1,0:T(8,128)(2,1)S(1)}, bf16[2048,128]{1,0:T(8,128)(2,1)S(1)}, u32[]{:S(2)}, u32[]{:S(2)}) collective-permute-start(bf16[2048,128]{1,0:T(8,128)(2,1)S(1)} %pad_maximum_fusion.refs_0_), channel_id=1, source_target_pairs={{0,1},{1,0},{2,3},{3,2},{4,5},{5,4},{6,7},{7,6},{8,9},{9,8},{10,11... | collective-permute-start | bytes 1572872 | tf_op jit(solution)/shard_map/ppermute | solution.py:199
  35.9 11.4 %all-to-all-start.1 = ((bf16[4,128,512]{1,2,0:T(8,128)(2,1)}), bf16[4,128,512]{1,2,0:T(8,128)(2,1)S(1)}, u32[]{:S(2)}, u32[]{:S(2)}) async-start(bf16[4,128,512]{1,2,0:T(8,128)(2,1)} %broadcast_in_dim.30), calls=%async_computation.1 | async-start | bytes 1048576 | tf_op jit(solution)/shard_map/all_to_all | solution.py:203
  40.7 7.3 %collective-permute-start.2 = (bf16[2048,128]{1,0:T(8,128)(2,1)S(1)}, bf16[2048,128]{1,0:T(8,128)(2,1)S(1)}, u32[]{:S(2)}, u32[]{:S(2)}) collective-permute-start(bf16[2048,128]{1,0:T(8,128)(2,1)S(1)} %collective-permute-done.1.refs_2_), channel_id=1, source_target_pairs={{0,1},{1,0},{2,3},{3,2},{4,5},{5,4},{6,7},{7,6},{8,9},{9,8},{10,11... | collective-permute-start | bytes 1572872 | tf_op jit(solution)/shard_map/ppermute | solution.py:199

commit v7 on v6

--- a/solution.py
+++ b/solution.py
@@ -226,7 +226,6 @@
     piece = memory.reshape(2, 2, 2, 2, 128).transpose(0, 1, 3, 2, 4).reshape(1, 16, 128)
     narrow = exchange(jnp.broadcast_to(piece, (32, 16, 128)), ("zh",) + BLOCK)
     narrow = narrow.reshape(4, 128, 128).transpose(1, 0, 2).reshape(1, 128, 512)
-    narrow, near, far = lax.optimization_barrier((narrow, near, far))
     weights = [own, near, far, swap(far, "c")]
     every = exchange(jnp.broadcast_to(narrow, (4, 128, 512)), "x")
     every, h, g, me = lax.optimization_barrier((every, h, g, jnp.stack([yl, c])))

time: 168 us -> 167 us (level)
  blocking collectives: 122 us -> 105 us
  starting transfers between devices: 18.5 us -> 29 us
  waiting for transfers between devices: 2.74 us -> 8.25 us
    all_to_all x7 -> x6, blocking collectives: 122 us -> 105 us  [exchange(): return lax.all_to_all(block, axes, split_axis=0, concat_axis=0, tiled=True)]
    all_to_all x1 -> x2, starting transfers between devices: 4.01 us -> 20.5 us  [exchange(): return lax.all_to_all(block, axes, split_axis=0, concat_axis=0, tiled=True)]
    ppermute x3, starting transfers between devices: 14.5 us -> 8.48 us  [swap(): return lax.ppermute(block, axis, [(0, 1), (1, 0)])]
    all_to_all x1 -> x2, waiting for transfers between devices: 2.74 us -> 7.52 us  [exchange(): return lax.all_to_all(block, axes, split_axis=0, concat_axis=0, tiled=True)]
  transfers between devices with their start and end apart: 4 -> 5, of which waited for: 1 -> 2; matrix products, arithmetic and copies ran while one was open for 1% -> 2% of each run, Pallas kernels for 0% -> 0%
where the time goes in v7:
time: 167 us; the launch traced here: 166 us
  blocking collectives  105 us (63%)
  starting transfers between devices  29 us (17%)
  Pallas kernels  15.6 us (9%)
  waiting for transfers between devices  8.25 us (5%)
  local copies, waits for them, and re-layouts  4.96 us (3%)
    all_to_all x6, blocking collectives, exchange(): return lax.all_to_all(block, axes, split_axis=0, concat_axis=0, tiled=True)  105 us
    all_to_all x2, starting transfers between devices, exchange(): return lax.all_to_all(block, axes, split_axis=0, concat_axis=0, tiled=True)  20.5 us
    pallas_call x1, Pallas kernels, chain(): pl.pallas_call(chain_kernel, out_shape=jax.ShapeDtypeStruct((SECTIONS, 8,...  14.2 us
    ppermute x3, starting transfers between devices, swap(): return lax.ppermute(block, axis, [(0, 1), (1, 0)])  8.48 us
    all_to_all x2, waiting for transfers between devices, exchange(): return lax.all_to_all(block, axes, split_axis=0, concat_axis=0, tiled=True)  7.52 us
  transfers between devices with their start and end apart: 5, of which 2 were waited for; matrix products, arithmetic and copies ran while one was open for 2% of the time, Pallas kernels for 0%

profile of v7, /device:TPU:1, one launch (start us, length us, event | category | flops | bytes accessed | tf_op | source)
XLA Modules:
  0.0 165.6 jit_solution(13858307171007263936)
XLA Ops:
  0.0 0.0 copy-start
  0.0 0.7 copy.22
  0.7 0.7 broadcast_in_dim.28
  1.4 16.5 %all-to-all-start = ((bf16[32,16,128]{2,1,0:T(8,128)(2,1)}), bf16[32,16,128]{2,1,0:T(8,128)(2,1)S(1)}, u32[]{:S(2)}, u32[]{:S(2)}) async-start(bf16[32,16,128]{2,1,0:T(8,128)(2,1)} %broadcast_in_dim.28), calls=%async_computation | async-start | bytes 262144 | tf_op jit(solution)/shard_map/all_to_all | solution.py:203
  17.9 0.0 copy-done
  17.9 0.0 copy-start.1
  18.0 0.3 copy.25
  18.2 0.7 copy-done.1
  18.9 0.3 copy.26
  19.2 0.3 pad_maximum_fusion.refs_0_
  19.5 2.3 %collective-permute-start.1 = (bf16[2048,128]{1,0:T(8,128)(2,1)S(1)}, bf16[2048,128]{1,0:T(8,128)(2,1)S(1)}, u32[]{:S(2)}, u32[]{:S(2)}) collective-permute-start(bf16[2048,128]{1,0:T(8,128)(2,1)S(1)} %pad_maximum_fusion.refs_0_), channel_id=1, source_target_pairs={{0,4},{4,0},{1,5},{5,1},{2,6},{6,2},{3,7},{7,3},{8,12},{12,8},{9,1... | collective-permute-start | bytes 1572872 | tf_op jit(solution)/shard_map/ppermute | solution.py:199
  21.8 7.5 %all-to-all-done = bf16[32,16,128]{2,1,0:T(8,128)(2,1)S(1)} async-done(((bf16[32,16,128]{2,1,0:T(8,128)(2,1)}), bf16[32,16,128]{2,1,0:T(8,128)(2,1)S(1)}, u32[]{:S(2)}, u32[]{:S(2)}) %all-to-all-start) | async-done | bytes 131104 | tf_op jit(solution)/shard_map/all_to_all | solution.py:203
  29.3 0.1 copy.23
  29.4 0.9 broadcast_in_dim.30
  30.3 4.0 %all-to-all-start.1 = ((bf16[4,128,512]{1,2,0:T(8,128)(2,1)}), bf16[4,128,512]{1,2,0:T(8,128)(2,1)S(1)}, u32[]{:S(2)}, u32[]{:S(2)}) async-start(bf16[4,128,512]{1,2,0:T(8,128)(2,1)} %broadcast_in_dim.30), calls=%async_computation.1 | async-start | bytes 1048576 | tf_op jit(solution)/shard_map/all_to_all | solution.py:203
  34.3 4.3 %collective-permute-start = (bf16[2048,128]{1,0:T(8,128)(2,1)S(1)}, bf16[2048,128]{1,0:T(8,128)(2,1)S(1)}, u32[]{:S(2)}, u32[]{:S(2)}) collective-permute-start(bf16[2048,128]{1,0:T(8,128)(2,1)S(1)} %pad_maximum_fusion.refs_0_), channel_id=1, source_target_pairs={{0,1},{1,0},{2,3},{3,2},{4,5},{5,4},{6,7},{7,6},{8,9},{9,8},{10,11... | collective-permute-start | bytes 1572872 | tf_op jit(solution)/shard_map/ppermute | solution.py:199
  38.6 0.8 dynamic-slice_bitcast_fusion
  39.4 0.1 pad_add_fusion.me_ref
  39.5 0.0 collective-permute-done.1.refs_2_
  39.5 1.9 %collective-permute-start.2 = (bf16[2048,128]{1,0:T(8,128)(2,1)S(1)}, bf16[2048,128]{1,0:T(8,128)(2,1)S(1)}, u32[]{:S(2)}, u32[]{:S(2)}) collective-permute-start(bf16[2048,128]{1,0:T(8,128)(2,1)S(1)} %collective-permute-done.1.refs_2_), channel_id=1, source_target_pairs={{0,1},{1,0},{2,3},{3,2},{4,5},{5,4},{6,7},{7,6},{8,9},{9,8},{10,11... | collective-permute-start | bytes 1572872 | tf_op jit(solution)/shard_map/ppermute | solution.py:199
  41.4 0.0 all-to-all-done.1
  41.5 0.4 convolution_convert_fusion.3
  41.8 0.4 convolution_convert_fusion.1
  42.2 0.0 collective-permute-done.refs_1_
  42.2 0.4 convolution_convert_fusion.2
  42.6 0.7 collective-permute-done.2.refs_3_
  43.3 0.4 broadcast_select_fusion.4
  43.8 0.1 copy.27
  43.9 19.4 %all_to_all.40 = bf16[32,8,512]{2,1,0:T(8,128)(2,1)S(1)} all-to-all(bf16[32,8,512]{2,1,0:T(8,128)(2,1)S(1)} %bitcast.50), channel_id=1, replica_groups=mesh['zh'=4,'x'=4,'yh'=4,'yl'=2,'zl'=2,'c'=2] {'zh','yh','zl'}, dimensions={0} | all-to-all | bytes 524288 | tf_op jit(solution)/shard_map/all_to_all | solution.py:203
  63.3 0.1 broadcast_in_dim.33
  63.4 15.9 %all_to_all.41 = bf16[4,4,8,8,512]{4,3,2,1,0:T(8,128)(2,1)S(1)} all-to-all(bf16[4,4,8,8,512]{4,3,2,1,0:T(8,128)(2,1)S(1)} %broadcast_in_dim.33), channel_id=1, replica_groups=mesh['zh'=4,'x'=4,'yh'=4,'yl'=2,'zl'=2,'c'=2] {'x'}, dimensions={0} | all-to-all | bytes 2097152 | tf_op jit(solution)/shard_map/all_to_all | solution.py:203
  79.3 14.2 %sections.1 = bf16[16,8,8,512]{3,2,1,0:T(8,128)(2,1)S(1)} custom-call(bf16[8,2048]{1,0:T(8,128)(2,1)S(1)} %get-tuple-element.10.h_ref, bf16[8,2048]{1,0:T(8,128)(2,1)S(1)} %get-tuple-element.11.g_ref, bf16[16,8,8,512]{3,2,1,0:T(8,128)(2,1)S(1)} %bitcast.39), custom_call_target="tpu_custom_call" | custom-call | tf_op jit(solution)/shard_map/sections/pallas_call | solution.py:137
  93.5 13.6 %all_to_all.42 = bf16[4,4,8,8,512]{4,3,2,1,0:T(8,128)(2,1)S(1)} all-to-all(bf16[4,4,8,8,512]{4,3,2,1,0:T(8,128)(2,1)S(1)} %bitcast.40), channel_id=1, replica_groups=mesh['zh'=4,'x'=4,'yh'=4,'yl'=2,'zl'=2,'c'=2] {'x'}, dimensions={0} | all-to-all | bytes 2097152 | tf_op jit(solution)/shard_map/all_to_all | solution.py:203
  107.1 0.2 reduce_sum.33
  107.3 0.1 reshape.51
  107.4 28.4 %all_to_all.43 = bf16[128,2,512]{2,1,0:T(2,128)(2,1)S(1)} all-to-all(bf16[128,2,512]{2,1,0:T(2,128)(2,1)S(1)} %reshape.51), channel_id=1, replica_groups=mesh['zh'=4,'x'=4,'yh'=4,'yl'=2,'zl'=2,'c'=2] {'zh','yh','zl','yl','c'}, dimensions={0} | all-to-all | bytes 524288 | tf_op jit(solution)/shard_map/all_to_all | solution.py:203
  135.9 0.1 reshape.52.part_ref
  136.0 1.4 term.1
  137.4 10.7 %all_to_all.44 = bf16[4,32,16,128]{3,2,1,0:T(8,128)(2,1)S(1)} all-to-all(bf16[4,32,16,128]{3,2,1,0:T(8,128)(2,1)S(1)} %bitcast.41), channel_id=1, replica_groups=mesh['zh'=4,'x'=4,'yh'=4,'yl'=2,'zl'=2,'c'=2] {'x'}, dimensions={0} | all-to-all | bytes 1048576 | tf_op jit(solution)/shard_map/all_to_all | solution.py:203
  148.1 0.1 reduce_sum.34
  148.2 16.8 %all_to_all.45 = bf16[32,16,128]{2,1,0:T(8,128)(2,1)S(1)} all-to-all(bf16[32,16,128]{2,1,0:T(8,128)(2,1)S(1)} %reduce_sum.34), channel_id=1, replica_groups=mesh['zh'=4,'x'=4,'yh'=4,'yl'=2,'zl'=2,'c'=2] {'zh','yh','zl'}, dimensions={0} | all-to-all | bytes 262144 | tf_op jit(solution)/shard_map/all_to_all | solution.py:203
  164.9 0.6 convert_reduce_fusion
  (11 shorter events, 0.1 us)
Async XLA Ops:
  0.0 17.9 %copy-start = (bf16[1,2048,64]{1,2,0:T(8,128)(2,1)S(1)}, bf16[1,2048,64]{1,2,0:T(8,128)(2,1)}, u32[]{:S(2)}) copy-start(bf16[1,2048,64]{1,2,0:T(8,128)(2,1)} %param.7) | copy-start | bytes 786436
  1.4 27.9 %all-to-all-start = ((bf16[32,16,128]{2,1,0:T(8,128)(2,1)}), bf16[32,16,128]{2,1,0:T(8,128)(2,1)S(1)}, u32[]{:S(2)}, u32[]{:S(2)}) async-start(bf16[32,16,128]{2,1,0:T(8,128)(2,1)} %broadcast_in_dim.28), calls=%async_computation | async-start | bytes 262144 | tf_op jit(solution)/shard_map/all_to_all | solution.py:203
  17.9 1.0 copy-start.1
  19.5 20.0 %collective-permute-start.1 = (bf16[2048,128]{1,0:T(8,128)(2,1)S(1)}, bf16[2048,128]{1,0:T(8,128)(2,1)S(1)}, u32[]{:S(2)}, u32[]{:S(2)}) collective-permute-start(bf16[2048,128]{1,0:T(8,128)(2,1)S(1)} %pad_maximum_fusion.refs_0_), channel_id=1, source_target_pairs={{0,4},{4,0},{1,5},{5,1},{2,6},{6,2},{3,7},{7,3},{8,12},{12,8},{9,1... | collective-permute-start | bytes 1572872 | tf_op jit(solution)/shard_map/ppermute | solution.py:199
  30.3 11.1 %all-to-all-start.1 = ((bf16[4,128,512]{1,2,0:T(8,128)(2,1)}), bf16[4,128,512]{1,2,0:T(8,128)(2,1)S(1)}, u32[]{:S(2)}, u32[]{:S(2)}) async-start(bf16[4,128,512]{1,2,0:T(8,128)(2,1)} %broadcast_in_dim.30), calls=%async_computation.1 | async-start | bytes 1048576 | tf_op jit(solution)/shard_map/all_to_all | solution.py:203
  34.3 7.9 %collective-permute-start = (bf16[2048,128]{1,0:T(8,128)(2,1)S(1)}, bf16[2048,128]{1,0:T(8,128)(2,1)S(1)}, u32[]{:S(2)}, u32[]{:S(2)}) collective-permute-start(bf16[2048,128]{1,0:T(8,128)(2,1)S(1)} %pad_maximum_fusion.refs_0_), channel_id=1, source_target_pairs={{0,1},{1,0},{2,3},{3,2},{4,5},{5,4},{6,7},{7,6},{8,9},{9,8},{10,11... | collective-permute-start | bytes 1572872 | tf_op jit(solution)/shard_map/ppermute | solution.py:199
  39.5 3.8 %collective-permute-start.2 = (bf16[2048,128]{1,0:T(8,128)(2,1)S(1)}, bf16[2048,128]{1,0:T(8,128)(2,1)S(1)}, u32[]{:S(2)}, u32[]{:S(2)}) collective-permute-start(bf16[2048,128]{1,0:T(8,128)(2,1)S(1)} %collective-permute-done.1.refs_2_), channel_id=1, source_target_pairs={{0,1},{1,0},{2,3},{3,2},{4,5},{5,4},{6,7},{7,6},{8,9},{9,8},{10,11... | collective-permute-start | bytes 1572872 | tf_op jit(solution)/shard_map/ppermute | solution.py:199
